TPU v7x, 32 devices: a whole 2x2x4 slice. The times are simulated.
32 devices in a mesh: grp: 2 (over y), dp: 4 (over z), mod: 2 (over x), rep: 2 (over core).
Axes of the slice: x: 2, y: 2, z: 4, core: 2. Of those that a mesh axis runs over, the one named last changes fastest.
Arguments:
- activations: bfloat16 [2, 8, 1024, 4096], P('mod', ('grp', 'dp'), 'rep'), parts along dimension 1, may hold values from -6 to 6
- out_grads: bfloat16 [2, 8, 1024, 4096], P('mod', ('grp', 'dp'), 'rep'), parts along dimension 1, may hold values from -0.1875 to 0.1875
- proj_in: bfloat16 [2, 32, 4096], P('mod'), may hold values from -0.09375 to 0.09375
- proj_out: bfloat16 [2, 32, 4096], P('mod'), may hold values from -0.09375 to 0.09375
- seq_lengths: int32 [8], P(('grp', 'dp')), parts along dimension 0, may hold values from 256 to 1024, as said below
- fisher_prior: float32 [2, 16, 1024, 1024], P('mod', ('grp', 'dp', 'rep')), parts along dimension 1, may hold values from -160 to 160, as said below
- query_grads: bfloat16 [2, 2, 512, 1024], P('mod', 'rep', 'dp'), may hold values from -32 to 32
Outputs:
- influence: float32 [8, 1024], P(('grp', 'dp'), 'rep'), parts along dimension 0
There are 2 independent parts, one for each index of `grp`. A program takes and returns all parts, laid end to end along the dimension named above; an argument that names none is the same for every part. Nothing has to cross between parts.
Inputs may be any that keep to these rules, and one draw needn't show every extreme that they name: `seq_lengths`: tokens of a sequence at positions from its length on do not count; in every draw some sequence has all 1024 tokens. `fisher_prior`: each partial is symmetric positive definite.
All inputs are finite; a program needn't handle non-finite values.
Results may differ from a plain program's by a relative error of at most 0.0003.
Values may be sent and summed in bfloat16 or wider, within the bound.
No kernel may reach another device: no remote copies, remote signals or barrier semaphores. Data moves between devices by JAX's collectives and lax.ppermute only.
A program may use at most 128 MiB of HBM per device.

v0:
```python
import functools

import jax
import jax.numpy as jnp
from jax import lax
from jax.experimental import pallas as pl
from jax.experimental.pallas import tpu as pltpu
from jax.sharding import PartitionSpec as P

damping_frac = 0.01
NB = 128
LANES = 128
SUB = 8
HEIGHTS = (1, 2, 2, 2, 1)
STARTS = tuple(sum(HEIGHTS[:c]) for c in range(len(HEIGHTS)))
HIGH = lax.Precision.HIGHEST


def iota(shape, dim):
    return lax.broadcasted_iota(jnp.int32, shape, dim)


def dot(a, b, dims, precision=HIGH):
    return lax.dot_general(
        a, b, (dims, ((), ())), precision=precision, preferred_element_type=jnp.float32
    )


def split(x):
    one = x.astype(jnp.bfloat16)
    x = x - one.astype(jnp.float32)
    two = x.astype(jnp.bfloat16)
    three = (x - two.astype(jnp.float32)).astype(jnp.bfloat16)
    return one, two, three


def left_terms(x):
    one, two, three = split(x)
    return jnp.concatenate([one, one, two, two, one, three], axis=1)


def right_terms(x):
    one, two, three = split(x)
    return jnp.concatenate([one, two, one, two, three, one], axis=1)


def three_terms(x):
    return jnp.concatenate(split(x), axis=1)


def right_six(x):
    one, two, three = x[:, :NB], x[:, NB : 2 * NB], x[:, 2 * NB :]
    return jnp.concatenate([one, two, one, two, three, one], axis=1)


def by_rows(a, b):
    return dot(a, b, ((1,), (1,)), None)


def project_kernel(steps, seqs, place_ref, act_ref, grad_ref, pin_ref, pout_ref, prior_ref, out_ref, ins, outs, tr):
    step = pl.program_id(0)
    in_side = by_rows(act_ref[0, 0], pin_ref[0])
    out_side = by_rows(grad_ref[0, 0], pout_ref[0])
    block = prior_ref[0, 0]
    on_diag = iota(block.shape, 0) == iota(block.shape, 1)
    line = jnp.sum(jnp.where(on_diag, block, 0.0), axis=0, keepdims=True)
    line = sum(line[:, c : c + LANES] for c in range(0, block.shape[1], LANES))

    @pl.when(step == 0)
    def _():
        ins[...] = in_side
        outs[...] = out_side
        tr[...] = jnp.zeros_like(tr)
        tr[0:1, :] = line
        out_ref[out_ref.shape[0] - NB :, :] = block[0:NB, 0:NB]

    @pl.when(step > 0)
    def _():
        ins[...] += in_side
        outs[...] += out_side
        tr[0:1, :] += line

    @pl.when(step == steps - 1)
    def _():
        rank = ins.shape[1]
        fold = LANES // rank
        rows = rank // fold
        token = place_ref[0] + iota(outs.shape, 0)
        kept = jnp.where(token < place_ref[1], outs[...], 0.0)
        matrix = dot(kept, ins[...], ((0,), (0,)))
        matrix = jnp.concatenate([matrix] * fold, axis=1)
        o = iota((rank, LANES), 0)
        lane = iota((rank, LANES), 1)
        matrix = jnp.where(lax.rem(o, fold) == lane // rank, matrix, 0.0)
        pick = (iota((rows, rank), 1) // fold == iota((rows, rank), 0)).astype(jnp.float32)
        vector = dot(pick, matrix, ((1,), (0,)))
        for s in range(seqs):
            out_ref[s * rows : (s + 1) * rows, :] = jnp.where(place_ref[2] == s, vector, 0.0)
        out_ref[seqs * rows : (seqs + 1) * rows, :] = tr[...]


def project(place, seqs, activations, out_grads, proj_in, proj_out, fisher_prior):
    steps = 4
    tok, width = activations.shape[2:]
    rank = proj_in.shape[1]
    size = fisher_prior.shape[2]
    part, blk = width // steps, size // steps
    rows = size // LANES
    height = (seqs + 1) * rows + NB
    return pl.pallas_call(
        functools.partial(project_kernel, steps, seqs),
        grid=(steps,),
        in_specs=[
            pl.BlockSpec(memory_space=pltpu.SMEM),
            pl.BlockSpec((1, 1, tok, part), lambda i: (0, 0, 0, i)),
            pl.BlockSpec((1, 1, tok, part), lambda i: (0, 0, 0, i)),
            pl.BlockSpec((1, rank, part), lambda i: (0, 0, i)),
            pl.BlockSpec((1, rank, part), lambda i: (0, 0, i)),
            pl.BlockSpec((1, 1, blk, blk), lambda i: (0, 0, i, i)),
        ],
        out_specs=pl.BlockSpec((height, LANES), lambda i: (0, 0)),
        out_shape=jax.ShapeDtypeStruct((height, LANES), jnp.float32),
        scratch_shapes=[
            pltpu.VMEM((tok, rank), jnp.float32),
            pltpu.VMEM((tok, rank), jnp.float32),
            pltpu.VMEM((rows, LANES), jnp.float32),
        ],
        compiler_params=pltpu.CompilerParams(vmem_limit_bytes=60 << 20),
        name="project",
    )(place, activations, out_grads, proj_in, proj_out, fisher_prior)


def reciprocal(p):
    return pl.reciprocal(p, approx=True)


def spread(x, k):
    return jnp.broadcast_to(x[k : k + 1, :], x.shape)


def lanes_of(x, k):
    return jnp.broadcast_to(x[:, k : k + 1], x.shape)


def solve_group(s, sets):
    s = [list(row) for row in s]
    sets = [list(x) for x in sets]
    scaled = [[None] * SUB for _ in sets]
    pairs = []
    for k in range(0, SUB, 2):
        a, b, c = s[k][k], s[k + 1][k], s[k + 1][k + 1]
        r = reciprocal(a * c - b * b)
        rest = range(k + 2, SUB)
        m = {i: s[i][k] * c - s[i][k + 1] * b for i in rest}
        n = {i: s[i][k + 1] * a - s[i][k] * b for i in rest}
        for i in rest:
            for j in range(k + 2, i + 1):
                s[i][j] = s[i][j] - (m[i] * s[j][k] + n[i] * s[j][k + 1]) * r
        m = {i: m[i] * r for i in rest}
        n = {i: n[i] * r for i in rest}
        for x, y in zip(sets, scaled):
            y[k], y[k + 1] = (c * x[k] - b * x[k + 1]) * r, (a * x[k + 1] - b * x[k]) * r
            for i in rest:
                x[i] = x[i] - (m[i] * x[k] + n[i] * x[k + 1])
        pairs.append((m, n))
    return sets, scaled, pairs


def back_group(w, pairs):
    w = list(w)
    for k in range(SUB - 4, -1, -2):
        m, n = pairs[k // 2]
        for i in range(SUB - 2, k, -2):
            w[k] = w[k] - (m[i] * w[i] + m[i + 1] * w[i + 1])
            w[k + 1] = w[k + 1] - (n[i] * w[i] + n[i + 1] * w[i + 1])
    return w


def less_products(x, a, b):
    early = (a[0] * b[0] + a[1] * b[1]) + (a[2] * b[2] + a[3] * b[3])
    return (x - early) - (a[4] * b[4] + a[5] * b[5]) - (a[6] * b[6] + a[7] * b[7])


def eliminate(rows):
    groups = len(rows)
    rows = list(rows)
    sub = iota((SUB, LANES), 0)
    lane = iota((SUB, LANES), 1)
    lower, scaled_rows = [], []
    cols = [lanes_of(rows[0], j) for j in range(SUB)]
    for g in range(groups):
        first = g * SUB
        here = (lane >= first) & (lane < first + SUB)
        unit = (lane - first == sub).astype(jnp.float32)
        s = [[spread(cols[j], i) for j in range(i + 1)] for i in range(SUB)]
        work = jnp.where(here, unit, rows[g])
        lower.append(jnp.where(lane < first + SUB, work, 0.0))
        near = list(range(g + 1, min(g + 3, groups)))
        sets = [[lanes_of(rows[h], first + j) for j in range(SUB)] for h in near]
        if near:
            ahead = [lanes_of(rows[g + 1], first + SUB + j) for j in range(SUB)]
        sets, scaled, pairs = solve_group(s, sets + [[spread(work, i) for i in range(SUB)]])
        if near:
            cols = [less_products(ahead[j], sets[0], [spread(d, j) for d in scaled[0]]) for j in range(SUB)]
        for h, x in zip(near, sets):
            rows[h] = less_products(jnp.where(here, 0.0, rows[h]), x, scaled[-1])
        picks = back_group(scaled[-1], pairs)
        work = picks[0]
        for i in range(1, SUB):
            work = jnp.where(sub == i, picks[i], work)
        scaled_rows.append(jnp.where(lane < first + SUB, work, 0.0))
        for h in range(g + 3, groups):
            x = [lanes_of(rows[h], first + j) for j in range(SUB)]
            rows[h] = less_products(jnp.where(here, 0.0, rows[h]), x[::-1], picks[::-1])
    return lower, scaled_rows


def owner(k):
    return max(b for b in range(len(STARTS)) if STARTS[b] <= k)


def y_rows(b, k):
    return HEIGHTS[b] * 2 * NB + k * HEIGHTS[b] * NB


def panel_kernel(c, size, seqs, padded, *refs):
    refs = list(refs)
    tall, done = HEIGHTS[c] * NB, STARTS[c] * NB
    wide = done + tall
    last = wide == size
    waits = {}

    def start(name, source, target, sem):
        waits[name] = pltpu.make_async_copy(source, target, sem)
        waits[name].start()

    def wait(name):
        if name in waits:
            waits.pop(name).wait()

    if c == 0:
        first_ref = refs.pop(0)
        head = first_ref.shape[0] - NB
        rows = size // LANES
    else:
        place_ref, half_ref, got_ref, half_other_ref, got_other_ref, aux_ref, x_ref = refs[:7]
        del refs[:7]
    kept = c + (c if last else 0)
    given = refs[:kept]
    del refs[:kept]
    if last:
        out_ref = refs.pop(0)
    else:
        if c == 0:
            aux_ref = refs.pop(0)
        x_out, terms_out, w_out = refs[:3]
        del refs[:3]
    p, ef, terms, sems = refs[:4]
    held = refs[4:]
    for b in range(kept):
        start(("terms", b) if b < c else ("w", b - c), given[b], held[b], sems.at[b])

    if c == 0:
        if padded > seqs:
            aux_ref[seqs:padded, :] = jnp.zeros((padded - seqs, size), jnp.float32)
        for r in range(seqs * rows):
            at = r % rows * LANES
            aux_ref[r // rows : r // rows + 1, at : at + LANES] = first_ref[r : r + 1, :]
        v = aux_ref[0:padded, :]
        trace = jnp.sum(first_ref[seqs * rows : head, :]) + jnp.sum(v * v)
        aux_ref[padded:, :] = size / jnp.broadcast_to(trace, (SUB, size))
    scale = aux_ref[padded : padded + 1, :]
    one, two, three = split(aux_ref[0:padded, 0:wide])
    outer_left = jnp.concatenate([x[:, done:] for x in (one, one, two, two, one, three)], axis=0)
    outer_right = jnp.concatenate([one, two, one, two, three, one], axis=0)
    if c == 0:
        p[0:NB, :] = first_ref[head:, :]
    else:
        rep, half = place_ref[0], tall // 2
        p[pl.ds(pl.multiple_of(rep * half, half), half), :] = half_ref[...] + got_ref[...]
        p[pl.ds(pl.multiple_of((1 - rep) * half, half), half), :] = half_other_ref[...] + got_other_ref[...]
    outer = dot(outer_left, outer_right, ((0,), (0,)), None)
    eye = iota((tall, wide), 0) + done == iota((tall, wide), 1)
    p[0:tall, :] = (p[0:tall, :] + outer) * scale[:, 0:wide] + jnp.where(eye, damping_frac, 0.0)
    if c:
        p[tall:, 0:done] = x_ref[...]
    p[tall:, done:] = aux_ref[0:padded, done:wide]

    for k in range(STARTS[c]):
        at, end = k * NB, (k + 1) * NB
        b = owner(k)
        wait(("terms", b))
        both = right_six(held[b][(k - STARTS[b]) * 2 * NB : (k - STARTS[b] + 1) * 2 * NB, :])
        y = by_rows(left_terms(p[0:tall, at:end]), both)
        p[0:tall, at:end] = y[:, NB:]
        left = left_terms(p[:, at:end])
        if not last:
            terms[y_rows(c, k) : y_rows(c, k) + tall, :] = three_terms(y[:, :NB])
        for b in range(owner(k), c):
            skip = max(k + 1 - STARTS[b], 0) * NB
            if skip < HEIGHTS[b] * NB:
                wait(("terms", b))
                cols = slice(STARTS[b] * NB + skip, (STARTS[b] + HEIGHTS[b]) * NB)
                right = right_six(held[b][y_rows(b, k) + skip : y_rows(b, k) + HEIGHTS[b] * NB, :])
                p[0:tall, cols] -= by_rows(left[0:tall], right)
        p[:, done:] -= by_rows(left, right_terms(y[:, :NB]))
    for i in range(HEIGHTS[c]):
        at, end = done + i * NB, done + (i + 1) * NB
        low, scl = eliminate([p[i * NB + r : i * NB + r + SUB, at:end] for r in range(0, NB, SUB)])
        for r in range(NB // SUB):
            ef[i, r * SUB : (r + 1) * SUB, :] = low[r]
            ef[i, NB + r * SUB : NB + (r + 1) * SUB, :] = scl[r]
        if not last:
            terms[i * 2 * NB : (i + 1) * 2 * NB, :] = three_terms(ef[i])
        both = right_terms(ef[i])
        rest = (i + 1) * NB
        y = by_rows(left_terms(p[rest:, at:end]), both)
        p[rest:, at:end] = y[:, NB:]
        if rest < tall:
            if not last:
                top = y_rows(c, STARTS[c] + i)
                terms[top : top + rest, :] = jnp.zeros((rest, 3 * NB), jnp.bfloat16)
                terms[top + rest : top + tall, :] = three_terms(y[0 : tall - rest, :NB])
            p[rest:, end:] -= by_rows(left_terms(y[:, NB:]), right_terms(y[0 : tall - rest, :NB]))
    if not last:
        x_out[...] = p[tall:, :]
        start("terms", terms, terms_out, sems.at[kept])
        start("w", p.at[0:tall, :], w_out, sems.at[kept + 1])
        wait("terms")
        wait("w")
        return
    for k in range(size // NB - 1, -1, -1):
        at, end = k * NB, (k + 1) * NB
        b = owner(k)
        i = k - STARTS[b]
        row = i * NB
        if b == c:
            e, w = ef[i, 0:NB, :], p[row : row + NB, 0:at]
        else:
            e = held[b][2 * row : 2 * row + NB, :].astype(jnp.float32)
            e = e[:, :NB] + e[:, NB : 2 * NB] + e[:, 2 * NB :]
            wait(("w", b))
            w = held[c + b][row : row + NB, 0:at]
        z = dot(p[tall:, at:end], e, ((1,), (0,)))
        p[tall:, at:end] = z
        if k:
            p[tall:, 0:at] -= dot(z, w, ((1,), (0,)))
    out_ref[...] = p[tall:, :] * scale


def panel(c, size, seqs, inputs, state):
    padded = -(-seqs // SUB) * SUB
    tall = HEIGHTS[c] * NB
    wide = STARTS[c] * NB + tall
    last = wide == size
    vmem, hbm = pl.BlockSpec(memory_space=pltpu.VMEM), pl.BlockSpec(memory_space=pltpu.HBM)
    shape = jax.ShapeDtypeStruct

    def terms_of(b):
        return y_rows(b, STARTS[b] + HEIGHTS[b] - 1), 3 * NB

    if last:
        outs, specs = [shape((padded, size), jnp.float32)], [vmem]
    else:
        outs = [
            shape((padded, wide), jnp.float32),
            shape(terms_of(c), jnp.bfloat16),
            shape((tall, wide), jnp.float32),
        ]
        specs = [vmem, hbm, hbm]
        if c == 0:
            outs, specs = [shape((padded + SUB, size), jnp.float32)] + outs, [vmem] + specs
    earlier = [terms for terms, _ in state] + ([w for _, w in state] if last else [])
    return pl.pallas_call(
        functools.partial(panel_kernel, c, size, seqs, padded),
        in_specs=([pl.BlockSpec(memory_space=pltpu.SMEM)] + [vmem] * 6 if c else [vmem]) + [hbm] * len(earlier),
        out_specs=specs,
        out_shape=outs,
        scratch_shapes=[
            pltpu.VMEM((tall + padded, wide), jnp.float32),
            pltpu.VMEM((HEIGHTS[c], 2 * NB, NB), jnp.float32),
            pltpu.VMEM(terms_of(0 if last else c), jnp.bfloat16),
            pltpu.SemaphoreType.DMA((len(earlier) + 2,)),
        ]
        + [pltpu.VMEM(x.shape, x.dtype) for x in earlier],
        compiler_params=pltpu.CompilerParams(vmem_limit_bytes=40 << 20),
        cost_estimate=pl.CostEstimate(flops=1_200_000_000, bytes_accessed=4_000_000, transcendentals=0),
        name="panel%d" % c,
    )(*inputs, *earlier)


def score_kernel(solved_ref, query_ref, out_ref):
    rows = solved_ref.shape[0]
    terms = by_rows(jnp.concatenate(split(solved_ref[...]), axis=0), query_ref[...])
    out_ref[...] = terms[0:rows] + terms[rows : 2 * rows] + terms[2 * rows :]


def score(solved, queries):
    vmem = pl.BlockSpec(memory_space=pltpu.VMEM)
    return pl.pallas_call(
        score_kernel,
        in_specs=[vmem, vmem],
        out_specs=vmem,
        out_shape=jax.ShapeDtypeStruct((solved.shape[0], queries.shape[0]), jnp.float32),
        name="score",
    )(solved, queries)


def after(x, *others):
    return lax.optimization_barrier((x,) + others)[0]


def inward(n):
    steps = [[(s, s + 1), (n - 1 - s, n - 2 - s)] for s in range(n // 2 - 1)]
    return steps + [[(n // 2 - 1, n // 2), (n // 2, n // 2 - 1)]] if n > 1 else []


def from_middle(x):
    n = lax.axis_size("dp")
    here = lax.axis_index("dp")
    for s in range(n // 2 - 2, -1, -1):
        got = lax.ppermute(x, "dp", [(s + 1, s), (n - 2 - s, n - 1 - s)])
        x = jnp.where((here == s) | (here == n - 1 - s), got, x)
    return x


SWAP = [(0, 1), (1, 0)]


def body(activations, out_grads, proj_in, proj_out, seq_lengths, fisher_prior, query_grads):
    tok_half = activations.shape[2]
    prior = fisher_prior[0, 0]
    size = prior.shape[0]
    seqs = lax.axis_size("dp")
    rep, dp = lax.axis_index("rep"), lax.axis_index("dp")
    count = len(HEIGHTS)
    steps = inward(seqs)

    def over_rep(c, gate):
        top, half = STARTS[c] * NB, HEIGHTS[c] * NB // 2
        wide = top + 2 * half
        array = prior if gate is None else after(prior, gate)
        other = lax.dynamic_slice(array, (top + (1 - rep) * half, 0), (half, wide))
        own = lax.dynamic_slice(array, (top + rep * half, 0), (half, wide))
        return own, lax.ppermute(other, "rep", SWAP)

    second = over_rep(1, None)
    place = jnp.stack([rep * tok_half, seq_lengths[0], dp]).astype(jnp.int32)
    first = project(place, seqs, activations, out_grads, proj_in, proj_out, fisher_prior)
    first = first + lax.ppermute(first, "rep", SWAP)
    swapped = came = first
    for i, step in enumerate(steps):
        first = first + lax.ppermute(first, "dp", step)
        if i == 0:
            came = first
    sums = [None, after(second[0] + second[1], came)]
    sums += [after(sum(over_rep(c, swapped)), came) for c in range(2, count)]
    aux, x_rows, *out = panel(0, size, seqs, [after(first, *sums[1:])], [])
    state, gates = [out], [aux]
    place = rep.astype(jnp.int32).reshape(1)

    def inwards(x, gate):
        for step in steps[:-1]:
            x = x + after(lax.ppermute(x, "dp", step), gate)
        return x

    inner = [None, inwards(sums[1], came), inwards(sums[2], gates[0])]
    for c in range(1, count):
        if c == 2:
            inner += [inwards(x, gates[1]) for x in sums[3:]]
        x = inner[c]
        got = lax.ppermute(x, "dp", steps[-1]) if steps else jnp.zeros_like(x)
        if c == count - 3:
            x = after(x, inner[-1])
        got = after(got, gates[c - 1])
        others = [lax.ppermute(half, "rep", SWAP) for half in (x, got)]
        out = panel(c, size, seqs, [place, x, got, *others, aux, x_rows], state)
        gates.append(out[0])
        if c == 2:
            queries = lax.all_gather(after(query_grads[0, 0], out[0]), "dp", axis=0, tiled=True)
        if c < count - 1:
            x_rows, *out = out
            state.append(out)
    scores = from_middle(score(out[0], queries))
    mine = lax.dynamic_slice(scores, (dp, 0), (1, scores.shape[1]))
    if lax.axis_size("mod") == 2:
        return mine + lax.ppermute(mine, "mod", SWAP)
    return lax.psum(mine, "mod")


def solution(mesh):
    placed = (
        P("mod", ("grp", "dp"), "rep", None),
        P("mod", ("grp", "dp"), "rep", None),
        P("mod", None, None),
        P("mod", None, None),
        P(("grp", "dp")),
        P("mod", ("grp", "dp", "rep"), None, None),
        P("mod", "rep", "dp", None),
    )
    return jax.shard_map(
        body, mesh=mesh, in_specs=placed, out_specs=P(("grp", "dp"), "rep"), check_vma=False
    )
```

profile of v0, /device:TPU:0, one launch (start us, length us, event | category | flops | bytes accessed | tf_op | source)
XLA Modules:
  0.0 158.7 jit_solution(4751296935305596574)
XLA Ops:
  7.2 0.6 pad_add_fusion.place_ref
  7.8 6.9 %project.1 = f32[168,128]{1,0:T(8,128)} custom-call(s32[3]{0:T(128)} %pad_add_fusion.place_ref, bf16[1,1,512,4096]{3,2,1,0:T(8,128)(2,1)} %act_ref.1, bf16[1,1,512,4096]{3,2,1,0:T(8,128)(2,1)} %grad_ref.1, bf16[1,32,4096]{2,1,0:T(8,128)(2,1)} %pin_ref.1, bf16[1,32,4096]{2,1,0:T(8,128)(2,1)} %pout_ref.1, f32[1,1,1024,1024]{3,2,1,0:T(8,128)} %prior_ref.1), custom_call_target="tpu_custom_call" | custom-call | tf_op jit(solution)/shard_map/project/pallas_call | solution.py:110
  14.7 0.4 collective-permute-start
  15.1 0.9 dynamic-slice_bitcast_fusion
  16.3 0.9 add.103
  17.2 4.9 %collective-permute-start.2 = (f32[168,128]{1,0:T(8,128)S(1)}, f32[168,128]{1,0:T(8,128)S(1)}, u32[]{:S(2)}, u32[]{:S(2)}) collective-permute-start(f32[168,128]{1,0:T(8,128)S(1)} %add.103), channel_id=1, source_target_pairs={{0,4},{12,8},{1,5},{13,9},{2,6},{14,10},{3,7},{15,11},{16,20},{28,... | collective-permute-start | bytes 258056 | tf_op jit(solution)/shard_map/ppermute | solution.py:453
  22.0 1.1 constant_dynamic-slice_fusion.2
  23.2 1.0 constant_dynamic-slice_fusion.4
  24.2 0.6 collective-permute-start.1
  24.7 1.0 constant_dynamic-slice_fusion.3
  25.8 0.7 collective-permute-start.7
  26.5 1.0 bitcast_add_fusion
  27.5 5.5 %collective-permute-start.5 = (f32[128,384]{1,0:T(8,128)S(1)}, f32[128,384]{1,0:T(8,128)S(1)}, u32[]{:S(2)}, u32[]{:S(2)}) collective-permute-start(f32[128,384]{1,0:T(8,128)S(1)} %bitcast_add_fusion), channel_id=1, source_target_pairs={{0,4},{12,8},{1,5},{13,9},{2,6},{14,10},{3,7},{15,11},{16,20},{28,... | collective-permute-start | bytes 589832 | tf_op jit(solution)/shard_map/ppermute | solution.py:464
  33.0 1.0 dynamic-slice_add_fusion.2
  34.0 2.3 %collective-permute-done.5 = f32[128,384]{1,0:T(8,128)S(1)} collective-permute-done((f32[128,384]{1,0:T(8,128)S(1)}, f32[128,384]{1,0:T(8,128)S(1)}, u32[]{:S(2)}, u32[]{:S(2)}) %collective-permute-start.5) | collective-permute-done | bytes 196640 | tf_op jit(solution)/shard_map/ppermute | solution.py:464
  36.3 0.7 collective-permute-start.6
  37.0 1.0 dynamic-slice_add_fusion.1
  38.0 6.1 %collective-permute-start.15 = (f32[128,640]{1,0:T(8,128)S(1)}, f32[128,640]{1,0:T(8,128)S(1)}, u32[]{:S(2)}, u32[]{:S(2)}) collective-permute-start(f32[128,640]{1,0:T(8,128)S(1)} %dynamic-slice_add_fusion.1), channel_id=1, source_target_pairs={{0,4},{12,8},{1,5},{13,9},{2,6},{14,10},{3,7},{15,11},{16,20},{28,... | collective-permute-start | bytes 983048 | tf_op jit(solution)/shard_map/ppermute | solution.py:464
  44.1 1.8 %dynamic-slice_add_fusion = f32[128,896]{1,0:T(8,128)} fusion(f32[128,896]{1,0:T(8,128)S(1)} %collective-permute-done.9, f32[1024,1024]{1,0:T(8,128)} %bitcast.14, s32[]{:T(128)S(6)} %select_n.42), kind=kLoop, calls=%fused_computation | loop fusion | flops 114688 | bytes 1376260 | tf_op jit(solution)/shard_map/add | solution.py:457
  46.0 3.5 %panel0.1 = (f32[16,1024]{1,0:T(8,128)S(1)}, f32[8,128]{1,0:T(8,128)S(1)}, bf16[256,384]{1,0:T(8,128)(2,1)S(1)}, f32[128,128]{1,0:T(8,128)S(1)}) custom-call(f32[168,128]{1,0:T(8,128)S(1)} %add.116.refs_0_), custom_call_target="tpu_custom_call" | custom-call | flops 1200000000 | bytes 4000000 | tf_op jit(solution)/shard_map/panel0/pallas_call | solution.py:374
  49.5 0.7 collective-permute-start.16
  50.3 0.5 collective-permute-start.11
  50.8 6.8 %collective-permute-start.3 = (f32[64,1024]{1,0:T(8,128)S(1)}, f32[64,1024]{1,0:T(8,128)S(1)}, u32[]{:S(2)}, u32[]{:S(2)}) collective-permute-start(f32[64,1024]{1,0:T(8,128)S(1)} %dynamic-slice_add_fusion.2), channel_id=1, source_target_pairs={{0,4},{12,8},{1,5},{13,9},{2,6},{14,10},{3,7},{15,11},{16,20},{28,... | collective-permute-start | bytes 786440 | tf_op jit(solution)/shard_map/ppermute | solution.py:464
  57.6 7.2 %panel1.1 = (f32[8,384]{1,0:T(8,128)S(1)}, bf16[1024,384]{1,0:T(8,128)(2,1)S(1)}, f32[256,384]{1,0:T(8,128)S(1)}) custom-call(s32[1]{0:T(128)} %bitcast.refs_0_, f32[128,384]{1,0:T(8,128)S(1)} %add.115.refs_1_, f32[128,384]{1,0:T(8,128)S(1)} %collective-permute-done.6.refs_2_, f32[128,384]{1,0:T(8,128)S(1)} %collective-permute-done.10.refs_3_, ...), custom_call_target="tpu_custom_call" | custom-call | flops 1200000000 | bytes 4000000 | tf_op jit(solution)/shard_map/panel1/pallas_call | solution.py:374
  64.9 0.5 collective-permute-start.18
  65.4 3.7 %collective-permute-start.13 = (f32[128,896]{1,0:T(8,128)}, f32[128,896]{1,0:T(8,128)}, u32[]{:S(2)}, u32[]{:S(2)}) collective-permute-start(f32[128,896]{1,0:T(8,128)} %dynamic-slice_add_fusion), channel_id=1, source_target_pairs={{0,4},{12,8},{1,5},{13,9},{2,6},{14,10},{3,7},{15,11},{16,20},{28,... | collective-permute-start | bytes 1376264 | tf_op jit(solution)/shard_map/ppermute | solution.py:464
  69.1 8.7 %panel2.1 = (f32[8,640]{1,0:T(8,128)S(1)}, bf16[1536,384]{1,0:T(8,128)(2,1)S(1)}, f32[256,640]{1,0:T(8,128)S(1)}) custom-call(s32[1]{0:T(128)} %bitcast.refs_0_, f32[128,640]{1,0:T(8,128)S(1)} %add.129.refs_1_, f32[128,640]{1,0:T(8,128)S(1)} %collective-permute-done.16.refs_2_, f32[128,640]{1,0:T(8,128)S(1)} %collective-permute-done.17.refs_3_, ...), custom_call_target="tpu_custom_call" | custom-call | flops 1200000000 | bytes 4000000 | tf_op jit(solution)/shard_map/panel2/pallas_call | solution.py:374
  77.8 0.6 copy-done.3
  78.6 1.2 add.128.refs_1_
  79.9 0.7 collective-permute-start.14
  80.6 0.5 collective-permute-start.20
  81.1 0.9 collective-permute-start.12
  82.2 0.3 collective-permute-done.19.refs_3_
  82.4 0.7 collective-permute-done.20.refs_4_
  83.1 0.7 copy-done.4
  83.8 10.3 %panel3.1 = (f32[8,896]{1,0:T(8,128)S(1)}, bf16[2048,384]{1,0:T(8,128)(2,1)S(1)}, f32[256,896]{1,0:T(8,128)S(1)}) custom-call(s32[1]{0:T(128)} %bitcast.refs_0_, f32[128,896]{1,0:T(8,128)S(1)} %add.128.refs_1_, f32[128,896]{1,0:T(8,128)S(1)} %collective-permute-done.14.refs_2_, f32[128,896]{1,0:T(8,128)S(1)} %collective-permute-done.19.refs_3_, ...), custom_call_target="tpu_custom_call" | custom-call | flops 1200000000 | bytes 4000000 | tf_op jit(solution)/shard_map/panel3/pallas_call | solution.py:374
  94.1 0.2 collective-permute-start.22
  94.3 1.4 collective-permute-done.22.refs_4_
  95.7 12.6 %panel4.1.solved_ref = f32[8,1024]{1,0:T(8,128)S(1)} custom-call(s32[1]{0:T(128)} %bitcast.refs_0_, f32[64,1024]{1,0:T(8,128)S(1)} %add.127.refs_1_, f32[64,1024]{1,0:T(8,128)S(1)} %collective-permute-done.12.refs_2_, f32[64,1024]{1,0:T(8,128)S(1)} %collective-permute-done.21.refs_3_, f32[64,1024]{1,0:T(8,128)S(1)} %collective-permute-done.22.refs_4_, ...), custom_call_target="tpu_custom_call" | custom-call | flops 1200000000 | bytes 4000000 | tf_op jit(solution)/shard_map/panel4/pallas_call | solution.py:374
  108.4 0.6 copy-done
  109.0 3.6 %all-gather.2.cloned.1.call-done.query_ref = bf16[512,1024]{1,0:T(8,128)(2,1)} async-done(((bf16[128,1024]{1,0:T(8,128)(2,1)}), bf16[512,1024]{1,0:T(8,128)(2,1)}) %all-gather.2.cloned.1.call-update) | async-done | bytes 1048592 | tf_op jit(solution)/shard_map/all_gather | solution.py:480
  112.6 2.3 %score.1 = f32[8,512]{1,0:T(8,128)} custom-call(f32[8,1024]{1,0:T(8,128)} %copy-done, bf16[512,1024]{1,0:T(8,128)(2,1)} %all-gather.2.cloned.1.call-done.query_ref), custom_call_target="tpu_custom_call" | custom-call | tf_op jit(solution)/shard_map/score/pallas_call | solution.py:400
  114.8 1.3 collective-permute-start.23
  116.1 30.8 %collective-permute-done.23 = f32[8,512]{1,0:T(8,128)S(1)} collective-permute-done((f32[8,512]{1,0:T(8,128)}, f32[8,512]{1,0:T(8,128)S(1)}, u32[]{:S(2)}, u32[]{:S(2)}) %collective-permute-start.23) | collective-permute-done | bytes 16416 | tf_op jit(solution)/shard_map/ppermute | solution.py:422
  146.9 0.7 broadcast_select_fusion
  147.6 1.2 collective-permute-start.24
  148.9 2.3 %collective-permute-done.24 = f32[1,512]{1,0:T(1,128)S(1)} collective-permute-done((f32[1,512]{1,0:T(1,128)S(1)}, f32[1,512]{1,0:T(1,128)S(1)}, u32[]{:S(2)}, u32[]{:S(2)}) %collective-permute-start.24) | collective-permute-done | bytes 2080 | tf_op jit(solution)/shard_map/ppermute | solution.py:487
  151.2 0.6 add.131
  (40 shorter events, 1.1 us)
Async XLA Ops:
  6.5 106.0 %all-gather.2.cloned.1.call-start = ((), (), s32[]{:S(2)}) async-start(), calls=%async_computation | async-start | bytes 1310720 | tf_op jit(solution)/shard_map/all_gather | solution.py:480
  14.7 1.6 %collective-permute-start = (f32[168,128]{1,0:T(8,128)}, f32[168,128]{1,0:T(8,128)S(1)}, u32[]{:S(2)}, u32[]{:S(2)}) collective-permute-start(f32[168,128]{1,0:T(8,128)} %project.1), channel_id=1, source_target_pairs={{0,1},{1,0},{2,3},{3,2},{4,5},{5,4},{6,7},{7,6},{8,9},{9,8},{10,11... | collective-permute-start | bytes 258056 | tf_op jit(solution)/shard_map/ppermute | solution.py:450
  16.1 10.4 %collective-permute-start.4 = (f32[128,384]{1,0:T(8,128)S(1)}, f32[128,384]{1,0:T(8,128)S(1)}, u32[]{:S(2)}, u32[]{:S(2)}) collective-permute-start(f32[128,384]{1,0:T(8,128)S(1)} %dynamic-slice_bitcast_fusion), channel_id=1, source_target_pairs={{0,1},{1,0},{2,3},{3,2},{4,5},{5,4},{6,7},{7,6},{8,9},{9,8},{10,11... | collective-permute-start | bytes 589832 | tf_op jit(solution)/shard_map/ppermute | solution.py:445
  17.2 8.6 %collective-permute-start.2 = (f32[168,128]{1,0:T(8,128)S(1)}, f32[168,128]{1,0:T(8,128)S(1)}, u32[]{:S(2)}, u32[]{:S(2)}) collective-permute-start(f32[168,128]{1,0:T(8,128)S(1)} %add.103), channel_id=1, source_target_pairs={{0,4},{12,8},{1,5},{13,9},{2,6},{14,10},{3,7},{15,11},{16,20},{28,... | collective-permute-start | bytes 258056 | tf_op jit(solution)/shard_map/ppermute | solution.py:453
  23.1 21.0 %collective-permute-start.9 = (f32[128,896]{1,0:T(8,128)S(1)}, f32[128,896]{1,0:T(8,128)S(1)}, u32[]{:S(2)}, u32[]{:S(2)}) collective-permute-start(f32[128,896]{1,0:T(8,128)S(1)} %constant_dynamic-slice_fusion.2), channel_id=1, source_target_pairs={{0,1},{1,0},{2,3},{3,2},{4,5},{5,4},{6,7},{7,6},{8,9},{9,8},{10,11... | collective-permute-start | bytes 1376264 | tf_op jit(solution)/shard_map/ppermute | solution.py:445
  24.2 8.9 %collective-permute-start.1 = (f32[64,1024]{1,0:T(8,128)S(1)}, f32[64,1024]{1,0:T(8,128)S(1)}, u32[]{:S(2)}, u32[]{:S(2)}) collective-permute-start(f32[64,1024]{1,0:T(8,128)S(1)} %constant_dynamic-slice_fusion.4), channel_id=1, source_target_pairs={{0,1},{1,0},{2,3},{3,2},{4,5},{5,4},{6,7},{7,6},{8,9},{9,8},{10,11... | collective-permute-start | bytes 786440 | tf_op jit(solution)/shard_map/ppermute | solution.py:445
  25.7 11.3 %collective-permute-start.8 = (f32[128,640]{1,0:T(8,128)S(1)}, f32[128,640]{1,0:T(8,128)S(1)}, u32[]{:S(2)}, u32[]{:S(2)}) collective-permute-start(f32[128,640]{1,0:T(8,128)S(1)} %constant_dynamic-slice_fusion.3), channel_id=1, source_target_pairs={{0,1},{1,0},{2,3},{3,2},{4,5},{5,4},{6,7},{7,6},{8,9},{9,8},{10,11... | collective-permute-start | bytes 983048 | tf_op jit(solution)/shard_map/ppermute | solution.py:445
  25.8 7.2 %collective-permute-start.7 = (f32[168,128]{1,0:T(8,128)S(1)}, f32[168,128]{1,0:T(8,128)S(1)}, u32[]{:S(2)}, u32[]{:S(2)}) collective-permute-start(f32[168,128]{1,0:T(8,128)S(1)} %add.109), channel_id=1, source_target_pairs={{4,8},{8,4},{5,9},{9,5},{6,10},{10,6},{7,11},{11,7},{20,24},{24,20... | collective-permute-start | bytes 258056 | tf_op jit(solution)/shard_map/ppermute | solution.py:453
  27.5 8.8 %collective-permute-start.5 = (f32[128,384]{1,0:T(8,128)S(1)}, f32[128,384]{1,0:T(8,128)S(1)}, u32[]{:S(2)}, u32[]{:S(2)}) collective-permute-start(f32[128,384]{1,0:T(8,128)S(1)} %bitcast_add_fusion), channel_id=1, source_target_pairs={{0,4},{12,8},{1,5},{13,9},{2,6},{14,10},{3,7},{15,11},{16,20},{28,... | collective-permute-start | bytes 589832 | tf_op jit(solution)/shard_map/ppermute | solution.py:464
  36.3 14.0 %collective-permute-start.6 = (f32[128,384]{1,0:T(8,128)S(1)}, f32[128,384]{1,0:T(8,128)S(1)}, u32[]{:S(2)}, u32[]{:S(2)}) collective-permute-start(f32[128,384]{1,0:T(8,128)S(1)} %add.115.refs_1_), channel_id=1, source_target_pairs={{4,8},{8,4},{5,9},{9,5},{6,10},{10,6},{7,11},{11,7},{20,24},{24,20... | collective-permute-start | bytes 589832 | tf_op jit(solution)/shard_map/ppermute | solution.py:472
  38.0 11.4 %collective-permute-start.15 = (f32[128,640]{1,0:T(8,128)S(1)}, f32[128,640]{1,0:T(8,128)S(1)}, u32[]{:S(2)}, u32[]{:S(2)}) collective-permute-start(f32[128,640]{1,0:T(8,128)S(1)} %dynamic-slice_add_fusion.1), channel_id=1, source_target_pairs={{0,4},{12,8},{1,5},{13,9},{2,6},{14,10},{3,7},{15,11},{16,20},{28,... | collective-permute-start | bytes 983048 | tf_op jit(solution)/shard_map/ppermute | solution.py:464
  49.4 28.4 %copy-start.1 = (f32[128,128]{1,0:T(8,128)}, f32[128,128]{1,0:T(8,128)S(1)}, u32[]{:S(2)}) copy-start(f32[128,128]{1,0:T(8,128)S(1)} %get-tuple-element.58.refs_11_) | copy-start | bytes 196612
  49.5 15.4 %collective-permute-start.16 = (f32[128,640]{1,0:T(8,128)S(1)}, f32[128,640]{1,0:T(8,128)S(1)}, u32[]{:S(2)}, u32[]{:S(2)}) collective-permute-start(f32[128,640]{1,0:T(8,128)S(1)} %add.129.refs_1_), channel_id=1, source_target_pairs={{4,8},{8,4},{5,9},{9,5},{6,10},{10,6},{7,11},{11,7},{20,24},{24,20... | collective-permute-start | bytes 983048 | tf_op jit(solution)/shard_map/ppermute | solution.py:472
  50.2 7.4 %collective-permute-start.10 = (f32[128,384]{1,0:T(8,128)S(1)}, f32[128,384]{1,0:T(8,128)S(1)}, u32[]{:S(2)}, u32[]{:S(2)}) collective-permute-start(f32[128,384]{1,0:T(8,128)S(1)} %add.115.refs_1_), channel_id=1, source_target_pairs={{0,1},{1,0},{2,3},{3,2},{4,5},{5,4},{6,7},{7,6},{8,9},{9,8},{10,11... | collective-permute-start | bytes 589832 | tf_op jit(solution)/shard_map/ppermute | solution.py:476
  50.3 7.3 %collective-permute-start.11 = (f32[128,384]{1,0:T(8,128)S(1)}, f32[128,384]{1,0:T(8,128)S(1)}, u32[]{:S(2)}, u32[]{:S(2)}) collective-permute-start(f32[128,384]{1,0:T(8,128)S(1)} %collective-permute-done.6.refs_2_), channel_id=1, source_target_pairs={{0,1},{1,0},{2,3},{3,2},{4,5},{5,4},{6,7},{7,6},{8,9},{9,8},{10,11... | collective-permute-start | bytes 589832 | tf_op jit(solution)/shard_map/ppermute | solution.py:476
  50.8 14.0 %collective-permute-start.3 = (f32[64,1024]{1,0:T(8,128)S(1)}, f32[64,1024]{1,0:T(8,128)S(1)}, u32[]{:S(2)}, u32[]{:S(2)}) collective-permute-start(f32[64,1024]{1,0:T(8,128)S(1)} %dynamic-slice_add_fusion.2), channel_id=1, source_target_pairs={{0,4},{12,8},{1,5},{13,9},{2,6},{14,10},{3,7},{15,11},{16,20},{28,... | collective-permute-start | bytes 786440 | tf_op jit(solution)/shard_map/ppermute | solution.py:464
  64.8 4.3 %collective-permute-start.17 = (f32[128,640]{1,0:T(8,128)S(1)}, f32[128,640]{1,0:T(8,128)S(1)}, u32[]{:S(2)}, u32[]{:S(2)}) collective-permute-start(f32[128,640]{1,0:T(8,128)S(1)} %add.129.refs_1_), channel_id=1, source_target_pairs={{0,1},{1,0},{2,3},{3,2},{4,5},{5,4},{6,7},{7,6},{8,9},{9,8},{10,11... | collective-permute-start | bytes 983048 | tf_op jit(solution)/shard_map/ppermute | solution.py:476
  64.9 4.2 %collective-permute-start.18 = (f32[128,640]{1,0:T(8,128)S(1)}, f32[128,640]{1,0:T(8,128)S(1)}, u32[]{:S(2)}, u32[]{:S(2)}) collective-permute-start(f32[128,640]{1,0:T(8,128)S(1)} %collective-permute-done.16.refs_2_), channel_id=1, source_target_pairs={{0,1},{1,0},{2,3},{3,2},{4,5},{5,4},{6,7},{7,6},{8,9},{9,8},{10,11... | collective-permute-start | bytes 983048 | tf_op jit(solution)/shard_map/ppermute | solution.py:476
  65.4 13.3 %collective-permute-start.13 = (f32[128,896]{1,0:T(8,128)}, f32[128,896]{1,0:T(8,128)}, u32[]{:S(2)}, u32[]{:S(2)}) collective-permute-start(f32[128,896]{1,0:T(8,128)} %dynamic-slice_add_fusion), channel_id=1, source_target_pairs={{0,4},{12,8},{1,5},{13,9},{2,6},{14,10},{3,7},{15,11},{16,20},{28,... | collective-permute-start | bytes 1376264 | tf_op jit(solution)/shard_map/ppermute | solution.py:464
  77.8 0.6 copy-start.3
  78.4 17.3 %copy-start.2 = (f32[128,128]{1,0:T(8,128)S(1)}, f32[128,128]{1,0:T(8,128)}, u32[]{:S(2)}) copy-start(f32[128,128]{1,0:T(8,128)} %copy-done.1) | copy-start | bytes 196612
  79.9 0.8 collective-permute-start.14
  80.6 1.9 %collective-permute-start.19 = (f32[128,896]{1,0:T(8,128)S(1)}, f32[128,896]{1,0:T(8,128)S(1)}, u32[]{:S(2)}, u32[]{:S(2)}) collective-permute-start(f32[128,896]{1,0:T(8,128)S(1)} %add.128.refs_1_), channel_id=1, source_target_pairs={{0,1},{1,0},{2,3},{3,2},{4,5},{5,4},{6,7},{7,6},{8,9},{9,8},{10,11... | collective-permute-start | bytes 1376264 | tf_op jit(solution)/shard_map/ppermute | solution.py:476
  80.6 2.4 %collective-permute-start.20 = (f32[128,896]{1,0:T(8,128)S(1)}, f32[128,896]{1,0:T(8,128)S(1)}, u32[]{:S(2)}, u32[]{:S(2)}) collective-permute-start(f32[128,896]{1,0:T(8,128)S(1)} %collective-permute-done.14.refs_2_), channel_id=1, source_target_pairs={{0,1},{1,0},{2,3},{3,2},{4,5},{5,4},{6,7},{7,6},{8,9},{9,8},{10,11... | collective-permute-start | bytes 1376264 | tf_op jit(solution)/shard_map/ppermute | solution.py:476
  81.1 13.0 %collective-permute-start.12 = (f32[64,1024]{1,0:T(8,128)S(1)}, f32[64,1024]{1,0:T(8,128)S(1)}, u32[]{:S(2)}, u32[]{:S(2)}) collective-permute-start(f32[64,1024]{1,0:T(8,128)S(1)} %add.127.refs_1_), channel_id=1, source_target_pairs={{4,8},{8,4},{5,9},{9,5},{6,10},{10,6},{7,11},{11,7},{20,24},{24,20... | collective-permute-start | bytes 786440 | tf_op jit(solution)/shard_map/ppermute | solution.py:472
  82.0 12.3 %collective-permute-start.21 = (f32[64,1024]{1,0:T(8,128)S(1)}, f32[64,1024]{1,0:T(8,128)S(1)}, u32[]{:S(2)}, u32[]{:S(2)}) collective-permute-start(f32[64,1024]{1,0:T(8,128)S(1)} %add.127.refs_1_), channel_id=1, source_target_pairs={{0,1},{1,0},{2,3},{3,2},{4,5},{5,4},{6,7},{7,6},{8,9},{9,8},{10,11... | collective-permute-start | bytes 786440 | tf_op jit(solution)/shard_map/ppermute | solution.py:476
  83.1 0.7 copy-start.4
  94.1 1.6 %collective-permute-start.22 = (f32[64,1024]{1,0:T(8,128)S(1)}, f32[64,1024]{1,0:T(8,128)S(1)}, u32[]{:S(2)}, u32[]{:S(2)}) collective-permute-start(f32[64,1024]{1,0:T(8,128)S(1)} %collective-permute-done.12.refs_2_), channel_id=1, source_target_pairs={{0,1},{1,0},{2,3},{3,2},{4,5},{5,4},{6,7},{7,6},{8,9},{9,8},{10,11... | collective-permute-start | bytes 786440 | tf_op jit(solution)/shard_map/ppermute | solution.py:476
  108.4 0.6 copy-start
  114.8 32.1 %collective-permute-start.23 = (f32[8,512]{1,0:T(8,128)}, f32[8,512]{1,0:T(8,128)S(1)}, u32[]{:S(2)}, u32[]{:S(2)}) collective-permute-start(f32[8,512]{1,0:T(8,128)} %score.1), channel_id=1, source_target_pairs={{4,0},{8,12},{5,1},{9,13},{6,2},{10,14},{7,3},{11,15},{20,16},{24,... | collective-permute-start | bytes 49160 | tf_op jit(solution)/shard_map/ppermute | solution.py:422
  147.6 3.6 %collective-permute-start.24 = (f32[1,512]{1,0:T(1,128)S(1)}, f32[1,512]{1,0:T(1,128)S(1)}, u32[]{:S(2)}, u32[]{:S(2)}) collective-permute-start(f32[1,512]{1,0:T(1,128)S(1)} %broadcast_select_fusion), channel_id=1, source_target_pairs={{0,2},{2,0},{1,3},{3,1},{4,6},{6,4},{5,7},{7,5},{8,10},{10,8},{9,1... | collective-permute-start | bytes 6152 | tf_op jit(solution)/shard_map/ppermute | solution.py:487
Sparse Core Ops, SparseCore 0:
  78.6 33.9 all-gather.1
where the time goes:
time: 159 us
  Pallas kernels  51.4 us (32%)
  waiting for transfers between devices  41.6 us (26%)
  starting transfers between devices  36.4 us (23%)
  between operations  14.4 us (9%)
  other arithmetic  8.92 us (6%)
  local copies, waits for them, and re-layouts  5.9 us (4%)
    pallas_call x5, Pallas kernels, panel(): pl.pallas_call(functools.partial(panel_kernel, c, size, seqs, padded), in...  42.2 us
    ppermute x1, waiting for transfers between devices, from_middle(): got = lax.ppermute(x, 'dp', [(s + 1, s), (n - 2 - s, n - 1 - s)])  30.8 us
    ppermute x4, starting transfers between devices, inwards(): x = x + after(lax.ppermute(x, 'dp', step), gate)  22.1 us
    pallas_call x1, Pallas kernels, project(): pl.pallas_call(functools.partial(project_kernel, steps, seqs), grid=(step...  6.89 us
    ppermute x2, starting transfers between devices, body(): first = first + lax.ppermute(first, 'dp', step)  5.53 us
    dynamic_slice x4, local copies, waits for them, and re-layouts, over_rep(): other = lax.dynamic_slice(array, (top + (1 - rep) * half, 0), (half, wide))  3.97 us
    add x3, other arithmetic, body(): sums += [after(sum(over_rep(c, swapped)), came) for c in range(2, count)]  3.85 us
    all_gather x1, waiting for transfers between devices, body(): lax.all_gather(after(query_grads[0, 0], out[0]), 'dp', axis=0, tiled=True)  3.57 us
  transfers between devices with their start and end apart: 26, of which 9 were waited for; matrix products, arithmetic and copies ran while one was open for 7% of the time, Pallas kernels for 27%

commit v1 on v0

--- a/solution.py
+++ b/solution.py
@@ -389,21 +389,30 @@
     )(*inputs, *earlier)
 
 
-def score_kernel(solved_ref, query_ref, out_ref):
+def score_kernel(side_ref, solved_ref, *refs):
+    blocks, out_ref = refs[:-1], refs[-1]
     rows = solved_ref.shape[0]
-    terms = by_rows(jnp.concatenate(split(solved_ref[...]), axis=0), query_ref[...])
-    out_ref[...] = terms[0:rows] + terms[rows : 2 * rows] + terms[2 * rows :]
-
-
-def score(solved, queries):
+    half = max(len(blocks) // 2, 1)
+    count = blocks[0].shape[0]
+    solved = jnp.concatenate(split(solved_ref[...]), axis=0)
+    for i, block in enumerate(blocks):
+        terms = by_rows(solved, block[...])
+        low, high = half - 1 - i % half, (half + i % half) if len(blocks) > 1 else 0
+        right_side = side_ref[0] if i < half else 1 - side_ref[0]
+        at = pl.multiple_of((low + right_side * (high - low)) * count, LANES)
+        out_ref[:, pl.ds(at, count)] = terms[0:rows] + terms[rows : 2 * rows] + terms[2 * rows :]
+
+
+def score(side, solved, blocks):
     vmem = pl.BlockSpec(memory_space=pltpu.VMEM)
+    count = len(blocks) * blocks[0].shape[0]
     return pl.pallas_call(
         score_kernel,
-        in_specs=[vmem, vmem],
+        in_specs=[pl.BlockSpec(memory_space=pltpu.SMEM)] + [vmem] * (1 + len(blocks)),
         out_specs=vmem,
-        out_shape=jax.ShapeDtypeStruct((solved.shape[0], queries.shape[0]), jnp.float32),
+        out_shape=jax.ShapeDtypeStruct((solved.shape[0], count), jnp.float32),
         name="score",
-    )(solved, queries)
+    )(side, solved, *blocks)
 
 
 def after(x, *others):
@@ -455,33 +464,41 @@
             came = first
     sums = [None, after(second[0] + second[1], came)]
     sums += [after(sum(over_rep(c, swapped)), came) for c in range(2, count)]
-    aux, x_rows, *out = panel(0, size, seqs, [after(first, *sums[1:])], [])
+
+    def inwards(x, *gate):
+        for step in steps[:-1]:
+            x = x + after(lax.ppermute(x, "dp", step), *gate)
+        return x
+
+    inner = [None, inwards(sums[1], *sums[2:4])]
+    aux, x_rows, *out = panel(0, size, seqs, [after(first, inner[1])], [])
     state, gates = [out], [aux]
     place = rep.astype(jnp.int32).reshape(1)
 
-    def inwards(x, gate):
-        for step in steps[:-1]:
-            x = x + after(lax.ppermute(x, "dp", step), gate)
-        return x
-
-    inner = [None, inwards(sums[1], came), inwards(sums[2], gates[0])]
+    inner.append(inwards(sums[2], gates[0]))
     for c in range(1, count):
         if c == 2:
             inner += [inwards(x, gates[1]) for x in sums[3:]]
         x = inner[c]
         got = lax.ppermute(x, "dp", steps[-1]) if steps else jnp.zeros_like(x)
-        if c == count - 3:
-            x = after(x, inner[-1])
+        if c == 2:
+            x = after(x, *inner[3:])
         got = after(got, gates[c - 1])
         others = [lax.ppermute(half, "rep", SWAP) for half in (x, got)]
         out = panel(c, size, seqs, [place, x, got, *others, aux, x_rows], state)
         gates.append(out[0])
         if c == 2:
-            queries = lax.all_gather(after(query_grads[0, 0], out[0]), "dp", axis=0, tiled=True)
+            near = [after(query_grads[0, 0], out[0])]
+            for step in steps[:-1]:
+                near = near[:1] + [lax.ppermute(x, "dp", step) for x in near]
+        if c == 3 and steps:
+            near = list(lax.optimization_barrier((*near, out[0])))[:-1]
+            near += [lax.ppermute(x, "dp", steps[-1]) for x in near]
         if c < count - 1:
             x_rows, *out = out
             state.append(out)
-    scores = from_middle(score(out[0], queries))
+    side = (dp >= seqs // 2).astype(jnp.int32).reshape(1)
+    scores = from_middle(score(side, out[0], near))
     mine = lax.dynamic_slice(scores, (dp, 0), (1, scores.shape[1]))
     if lax.axis_size("mod") == 2:
         return mine + lax.ppermute(mine, "mod", SWAP)

time: 159 us -> 123 us (0.77)
  waiting for transfers between devices: 41.6 us -> 9.95 us
  between operations: 14.4 us -> 1.03 us
  local copies, waits for them, and re-layouts: 5.9 us -> 11.2 us
  starting transfers between devices: 36.4 us -> 40.4 us
  other arithmetic: 8.92 us -> 6.99 us
    ppermute x1, waiting for transfers between devices: 30.8 us -> 4.53 us  [from_middle(): got = lax.ppermute(x, 'dp', [(s + 1, s), (n - 2 - s, n - 1 - s)])]
    unnamed x10 -> x22, local copies, waits for them, and re-layouts: 1.93 us -> 7.24 us
    all_gather x1 -> x0, waiting for transfers between devices: 3.57 us -> none  [body(): lax.all_gather(after(query_grads[0, 0], out[0]), 'dp', axis=0, tiled=True)]
    ppermute x4 -> x7, starting transfers between devices: 22.1 us -> 25.5 us  [the longest x4 17 us: inwards(): x = x + after(lax.ppermute(x, 'dp', step), *gate)]
  transfers between devices with their start and end apart: 26 -> 28, of which waited for: 9 -> 6; matrix products, arithmetic and copies ran while one was open for 7% -> 7% of each run, Pallas kernels for 27% -> 35%
where the time goes in v1:
time: 123 us; the launch traced here: 122 us
  Pallas kernels  52.4 us (43%)
  starting transfers between devices  40.4 us (33%)
  local copies, waits for them, and re-layouts  11.2 us (9%)
  waiting for transfers between devices  9.95 us (8%)
  other arithmetic  6.99 us (6%)
    pallas_call x5, Pallas kernels, panel(): pl.pallas_call(functools.partial(panel_kernel, c, size, seqs, padded), in...  43.1 us
    ppermute x4, starting transfers between devices, inwards(): x = x + after(lax.ppermute(x, 'dp', step), *gate)  17 us
    unnamed x22, local copies, waits for them, and re-layouts  7.24 us
    pallas_call x1, Pallas kernels, project(): pl.pallas_call(functools.partial(project_kernel, steps, seqs), grid=(step...  7.03 us
    ppermute x1, starting transfers between devices, body(): near = near[:1] + [lax.ppermute(x, 'dp', step) for x in near]  5.8 us
    ppermute x2, starting transfers between devices, body(): first = first + lax.ppermute(first, 'dp', step)  5.54 us
    ppermute x1, waiting for transfers between devices, from_middle(): got = lax.ppermute(x, 'dp', [(s + 1, s), (n - 2 - s, n - 1 - s)])  4.53 us
    dynamic_slice x4, local copies, waits for them, and re-layouts, over_rep(): other = lax.dynamic_slice(array, (top + (1 - rep) * half, 0), (half, wide))  3.97 us
  transfers between devices with their start and end apart: 28, of which 6 were waited for; matrix products, arithmetic and copies ran while one was open for 7% of the time, Pallas kernels for 35%

profile of v1, /device:TPU:0, one launch (start us, length us, event | category | flops | bytes accessed | tf_op | source)
XLA Modules:
  0.0 122.0 jit_solution(4320007036222244938)
XLA Ops:
  0.7 0.6 pad_add_fusion.place_ref
  1.2 7.0 %project.1 = f32[168,128]{1,0:T(8,128)} custom-call(s32[3]{0:T(128)} %pad_add_fusion.place_ref, bf16[1,1,512,4096]{3,2,1,0:T(8,128)(2,1)} %act_ref.1, bf16[1,1,512,4096]{3,2,1,0:T(8,128)(2,1)} %grad_ref.1, bf16[1,32,4096]{2,1,0:T(8,128)(2,1)} %pin_ref.1, bf16[1,32,4096]{2,1,0:T(8,128)(2,1)} %pout_ref.1, f32[1,1,1024,1024]{3,2,1,0:T(8,128)} %prior_ref.1), custom_call_target="tpu_custom_call" | custom-call | tf_op jit(solution)/shard_map/project/pallas_call | solution.py:110
  8.7 0.9 dynamic-slice_bitcast_fusion
  9.8 0.9 add.103
  10.7 4.9 %collective-permute-start.2 = (f32[168,128]{1,0:T(8,128)S(1)}, f32[168,128]{1,0:T(8,128)S(1)}, u32[]{:S(2)}, u32[]{:S(2)}) collective-permute-start(f32[168,128]{1,0:T(8,128)S(1)} %add.103), channel_id=1, source_target_pairs={{0,4},{12,8},{1,5},{13,9},{2,6},{14,10},{3,7},{15,11},{16,20},{28,... | collective-permute-start | bytes 258056 | tf_op jit(solution)/shard_map/ppermute | solution.py:462
  15.6 1.1 constant_dynamic-slice_fusion.2
  16.7 1.0 constant_dynamic-slice_fusion.3
  17.8 0.6 collective-permute-start.6
  18.3 1.0 constant_dynamic-slice_fusion.4
  19.4 0.7 collective-permute-start.9
  20.1 1.0 bitcast_add_fusion
  21.0 5.5 %collective-permute-start.5 = (f32[128,384]{1,0:T(8,128)S(1)}, f32[128,384]{1,0:T(8,128)S(1)}, u32[]{:S(2)}, u32[]{:S(2)}) collective-permute-start(f32[128,384]{1,0:T(8,128)S(1)} %bitcast_add_fusion), channel_id=1, source_target_pairs={{0,4},{12,8},{1,5},{13,9},{2,6},{14,10},{3,7},{15,11},{16,20},{28,... | collective-permute-start | bytes 589832 | tf_op jit(solution)/shard_map/ppermute | solution.py:470
  26.6 1.0 dynamic-slice_add_fusion.1
  27.6 1.3 %collective-permute-start.15 = (f32[128,640]{1,0:T(8,128)S(1)}, f32[128,640]{1,0:T(8,128)S(1)}, u32[]{:S(2)}, u32[]{:S(2)}) collective-permute-start(f32[128,640]{1,0:T(8,128)S(1)} %dynamic-slice_add_fusion.1), channel_id=1, source_target_pairs={{0,4},{12,8},{1,5},{13,9},{2,6},{14,10},{3,7},{15,11},{16,20},{28,... | collective-permute-start | bytes 983048 | tf_op jit(solution)/shard_map/ppermute | solution.py:470
  28.9 1.1 dynamic-slice_add_fusion
  30.0 1.7 %collective-permute-done.5 = f32[128,384]{1,0:T(8,128)S(1)} collective-permute-done((f32[128,384]{1,0:T(8,128)S(1)}, f32[128,384]{1,0:T(8,128)S(1)}, u32[]{:S(2)}, u32[]{:S(2)}) %collective-permute-start.5) | collective-permute-done | bytes 196640 | tf_op jit(solution)/shard_map/ppermute | solution.py:470
  31.7 0.7 collective-permute-start.8
  32.5 6.1 %collective-permute-start.13 = (f32[128,896]{1,0:T(8,128)S(1)}, f32[128,896]{1,0:T(8,128)S(1)}, u32[]{:S(2)}, u32[]{:S(2)}) collective-permute-start(f32[128,896]{1,0:T(8,128)S(1)} %dynamic-slice_add_fusion), channel_id=1, source_target_pairs={{0,4},{12,8},{1,5},{13,9},{2,6},{14,10},{3,7},{15,11},{16,20},{28,... | collective-permute-start | bytes 1376264 | tf_op jit(solution)/shard_map/ppermute | solution.py:470
  38.6 3.5 %panel0.1 = (f32[16,1024]{1,0:T(8,128)S(1)}, f32[8,128]{1,0:T(8,128)S(1)}, bf16[256,384]{1,0:T(8,128)(2,1)S(1)}, f32[128,128]{1,0:T(8,128)S(1)}) custom-call(f32[168,128]{1,0:T(8,128)S(1)} %add.126.refs_0_), custom_call_target="tpu_custom_call" | custom-call | flops 1200000000 | bytes 4000000 | tf_op jit(solution)/shard_map/panel0/pallas_call | solution.py:374
  42.2 0.7 collective-permute-start.16
  43.1 1.0 dynamic-slice_add_fusion.2
  44.1 4.1 %collective-permute-start.3 = (f32[64,1024]{1,0:T(8,128)S(1)}, f32[64,1024]{1,0:T(8,128)S(1)}, u32[]{:S(2)}, u32[]{:S(2)}) collective-permute-start(f32[64,1024]{1,0:T(8,128)S(1)} %dynamic-slice_add_fusion.2), channel_id=1, source_target_pairs={{0,4},{12,8},{1,5},{13,9},{2,6},{14,10},{3,7},{15,11},{16,20},{28,... | collective-permute-start | bytes 786440 | tf_op jit(solution)/shard_map/ppermute | solution.py:470
  48.2 7.2 %panel1.1 = (f32[8,384]{1,0:T(8,128)S(1)}, bf16[1024,384]{1,0:T(8,128)(2,1)S(1)}, f32[256,384]{1,0:T(8,128)S(1)}) custom-call(s32[1]{0:T(128)} %bitcast.1.refs_0_, f32[128,384]{1,0:T(8,128)S(1)} %add.125.refs_1_, f32[128,384]{1,0:T(8,128)S(1)} %collective-permute-done.8.refs_2_, f32[128,384]{1,0:T(8,128)S(1)} %collective-permute-done.10.refs_3_, ...), custom_call_target="tpu_custom_call" | custom-call | flops 1200000000 | bytes 4000000 | tf_op jit(solution)/shard_map/panel1/pallas_call | solution.py:374
  55.5 0.9 collective-permute-start.14
  57.1 1.0 collective-permute-done.17.refs_3_
  58.6 8.7 %panel2.1 = (f32[8,640]{1,0:T(8,128)S(1)}, bf16[1536,384]{1,0:T(8,128)(2,1)S(1)}, f32[256,640]{1,0:T(8,128)S(1)}) custom-call(s32[1]{0:T(128)} %bitcast.1.refs_0_, f32[128,640]{1,0:T(8,128)S(1)} %add.129.refs_1_, f32[128,640]{1,0:T(8,128)S(1)} %collective-permute-done.16.refs_2_, f32[128,640]{1,0:T(8,128)S(1)} %collective-permute-done.17.refs_3_, ...), custom_call_target="tpu_custom_call" | custom-call | flops 1200000000 | bytes 4000000 | tf_op jit(solution)/shard_map/panel2/pallas_call | solution.py:374
  67.5 1.4 %collective-permute-start.12 = (f32[64,1024]{1,0:T(8,128)S(1)}, f32[64,1024]{1,0:T(8,128)}, u32[]{:S(2)}, u32[]{:S(2)}) collective-permute-start(f32[64,1024]{1,0:T(8,128)S(1)} %add.127.refs_1_), channel_id=1, source_target_pairs={{4,8},{8,4},{5,9},{9,5},{6,10},{10,6},{7,11},{11,7},{20,24},{24,20... | collective-permute-start | bytes 786440 | tf_op jit(solution)/shard_map/ppermute | solution.py:483
  68.8 5.8 %collective-permute-start.23 = (bf16[128,1024]{1,0:T(8,128)(2,1)}, bf16[128,1024]{1,0:T(8,128)(2,1)}, u32[]{:S(2)}, u32[]{:S(2)}) collective-permute-start(bf16[128,1024]{1,0:T(8,128)(2,1)} %bitcast.7.refs_0_), channel_id=1, source_target_pairs={{0,4},{12,8},{1,5},{13,9},{2,6},{14,10},{3,7},{15,11},{16,20},{28,... | collective-permute-start | bytes 786440 | tf_op jit(solution)/shard_map/ppermute | solution.py:493
  74.7 10.3 %panel3.1 = (f32[8,896]{1,0:T(8,128)S(1)}, bf16[2048,384]{1,0:T(8,128)(2,1)S(1)}, f32[256,896]{1,0:T(8,128)S(1)}) custom-call(s32[1]{0:T(128)} %bitcast.1.refs_0_, f32[128,896]{1,0:T(8,128)S(1)} %add.128.refs_1_, f32[128,896]{1,0:T(8,128)S(1)} %collective-permute-done.14.refs_2_, f32[128,896]{1,0:T(8,128)S(1)} %collective-permute-done.19.refs_3_, ...), custom_call_target="tpu_custom_call" | custom-call | flops 1200000000 | bytes 4000000 | tf_op jit(solution)/shard_map/panel3/pallas_call | solution.py:374
  85.0 0.9 copy-done
  86.0 0.6 copy-done.9
  86.6 0.5 collective-permute-start.22
  87.1 1.4 %collective-permute-start.24 = (bf16[128,1024]{1,0:T(8,128)(2,1)}, bf16[128,1024]{1,0:T(8,128)(2,1)}, u32[]{:S(2)}, u32[]{:S(2)}) collective-permute-start(bf16[128,1024]{1,0:T(8,128)(2,1)} %bitcast.7.refs_0_), channel_id=1, source_target_pairs={{4,8},{8,4},{5,9},{9,5},{6,10},{10,6},{7,11},{11,7},{20,24},{24,20... | collective-permute-start | bytes 786440 | tf_op jit(solution)/shard_map/ppermute | solution.py:496
  88.4 1.4 %collective-permute-start.25 = (bf16[128,1024]{1,0:T(8,128)(2,1)}, bf16[128,1024]{1,0:T(8,128)(2,1)}, u32[]{:S(2)}, u32[]{:S(2)}) collective-permute-start(bf16[128,1024]{1,0:T(8,128)(2,1)} %collective-permute-done.23.refs_1_), channel_id=1, source_target_pairs={{4,8},{8,4},{5,9},{9,5},{6,10},{10,6},{7,11},{11,7},{20,24},{24,20... | collective-permute-start | bytes 786440 | tf_op jit(solution)/shard_map/ppermute | solution.py:496
  89.8 1.2 copy-done.1
  91.0 1.1 copy-done.3
  92.1 1.1 copy-done.5
  93.2 0.9 copy-done.7
  94.2 0.7 copy-done.10
  94.9 13.5 %panel4.1.solved_ref = f32[8,1024]{1,0:T(8,128)S(1)} custom-call(s32[1]{0:T(128)} %bitcast.1.refs_0_, f32[64,1024]{1,0:T(8,128)S(1)} %add.127.refs_1_, f32[64,1024]{1,0:T(8,128)} %collective-permute-done.12.refs_2_, f32[64,1024]{1,0:T(8,128)} %collective-permute-done.21.refs_3_, f32[64,1024]{1,0:T(8,128)} %collective-permute-done.22.refs_4_, ...), custom_call_target="tpu_custom_call" | custom-call | flops 1200000000 | bytes 4000000 | tf_op jit(solution)/shard_map/panel4/pallas_call | solution.py:374
  108.4 0.6 copy-done.8
  109.0 2.3 %score.1 = f32[8,512]{1,0:T(8,128)} custom-call(s32[1]{0:T(128)} %bitcast.side_ref, f32[8,1024]{1,0:T(8,128)} %copy-done.8, bf16[128,1024]{1,0:T(8,128)(2,1)} %bitcast.7.refs_0_, bf16[128,1024]{1,0:T(8,128)(2,1)} %collective-permute-done.23.refs_1_, bf16[128,1024]{1,0:T(8,128)(2,1)} %collective-permute-done.24.refs_2_, ...), custom_call_target="tpu_custom_call" | custom-call | tf_op jit(solution)/shard_map/score/pallas_call | solution.py:409
  111.3 1.3 %collective-permute-start.26 = (f32[8,512]{1,0:T(8,128)}, f32[8,512]{1,0:T(8,128)S(1)}, u32[]{:S(2)}, u32[]{:S(2)}) collective-permute-start(f32[8,512]{1,0:T(8,128)} %score.1), channel_id=1, source_target_pairs={{4,0},{8,12},{5,1},{9,13},{6,2},{10,14},{7,3},{11,15},{20,16},{24,... | collective-permute-start | bytes 49160 | tf_op jit(solution)/shard_map/ppermute | solution.py:431
  112.6 4.5 %collective-permute-done.26 = f32[8,512]{1,0:T(8,128)S(1)} collective-permute-done((f32[8,512]{1,0:T(8,128)}, f32[8,512]{1,0:T(8,128)S(1)}, u32[]{:S(2)}, u32[]{:S(2)}) %collective-permute-start.26) | collective-permute-done | bytes 16416 | tf_op jit(solution)/shard_map/ppermute | solution.py:431
  117.1 0.7 broadcast_select_fusion
  117.8 1.5 %collective-permute-start.27 = (f32[1,512]{1,0:T(1,128)S(1)}, f32[1,512]{1,0:T(1,128)S(1)}, u32[]{:S(2)}, u32[]{:S(2)}) collective-permute-start(f32[1,512]{1,0:T(1,128)S(1)} %broadcast_select_fusion), channel_id=1, source_target_pairs={{0,2},{2,0},{1,3},{3,1},{4,6},{6,4},{5,7},{7,5},{8,10},{10,8},{9,1... | collective-permute-start | bytes 6152 | tf_op jit(solution)/shard_map/ppermute | solution.py:504
  119.3 2.1 %collective-permute-done.27 = f32[1,512]{1,0:T(1,128)S(1)} collective-permute-done((f32[1,512]{1,0:T(1,128)S(1)}, f32[1,512]{1,0:T(1,128)S(1)}, u32[]{:S(2)}, u32[]{:S(2)}) %collective-permute-start.27) | collective-permute-done | bytes 2080 | tf_op jit(solution)/shard_map/ppermute | solution.py:504
  121.4 0.6 add.131
  (55 shorter events, 2.7 us)
Async XLA Ops:
  8.2 1.6 %collective-permute-start = (f32[168,128]{1,0:T(8,128)}, f32[168,128]{1,0:T(8,128)S(1)}, u32[]{:S(2)}, u32[]{:S(2)}) collective-permute-start(f32[168,128]{1,0:T(8,128)} %project.1), channel_id=1, source_target_pairs={{0,1},{1,0},{2,3},{3,2},{4,5},{5,4},{6,7},{7,6},{8,9},{9,8},{10,11... | collective-permute-start | bytes 258056 | tf_op jit(solution)/shard_map/ppermute | solution.py:459
  9.6 10.4 %collective-permute-start.4 = (f32[128,384]{1,0:T(8,128)S(1)}, f32[128,384]{1,0:T(8,128)S(1)}, u32[]{:S(2)}, u32[]{:S(2)}) collective-permute-start(f32[128,384]{1,0:T(8,128)S(1)} %dynamic-slice_bitcast_fusion), channel_id=1, source_target_pairs={{0,1},{1,0},{2,3},{3,2},{4,5},{5,4},{6,7},{7,6},{8,9},{9,8},{10,11... | collective-permute-start | bytes 589832 | tf_op jit(solution)/shard_map/ppermute | solution.py:454
  10.7 8.6 %collective-permute-start.2 = (f32[168,128]{1,0:T(8,128)S(1)}, f32[168,128]{1,0:T(8,128)S(1)}, u32[]{:S(2)}, u32[]{:S(2)}) collective-permute-start(f32[168,128]{1,0:T(8,128)S(1)} %add.103), channel_id=1, source_target_pairs={{0,4},{12,8},{1,5},{13,9},{2,6},{14,10},{3,7},{15,11},{16,20},{28,... | collective-permute-start | bytes 258056 | tf_op jit(solution)/shard_map/ppermute | solution.py:462
  16.7 12.2 %collective-permute-start.7 = (f32[128,896]{1,0:T(8,128)S(1)}, f32[128,896]{1,0:T(8,128)S(1)}, u32[]{:S(2)}, u32[]{:S(2)}) collective-permute-start(f32[128,896]{1,0:T(8,128)S(1)} %constant_dynamic-slice_fusion.2), channel_id=1, source_target_pairs={{0,1},{1,0},{2,3},{3,2},{4,5},{5,4},{6,7},{7,6},{8,9},{9,8},{10,11... | collective-permute-start | bytes 1376264 | tf_op jit(solution)/shard_map/ppermute | solution.py:454
  17.8 8.8 %collective-permute-start.6 = (f32[128,640]{1,0:T(8,128)S(1)}, f32[128,640]{1,0:T(8,128)S(1)}, u32[]{:S(2)}, u32[]{:S(2)}) collective-permute-start(f32[128,640]{1,0:T(8,128)S(1)} %constant_dynamic-slice_fusion.3), channel_id=1, source_target_pairs={{0,1},{1,0},{2,3},{3,2},{4,5},{5,4},{6,7},{7,6},{8,9},{9,8},{10,11... | collective-permute-start | bytes 983048 | tf_op jit(solution)/shard_map/ppermute | solution.py:454
  19.3 23.9 %collective-permute-start.1 = (f32[64,1024]{1,0:T(8,128)S(1)}, f32[64,1024]{1,0:T(8,128)S(1)}, u32[]{:S(2)}, u32[]{:S(2)}) collective-permute-start(f32[64,1024]{1,0:T(8,128)S(1)} %constant_dynamic-slice_fusion.4), channel_id=1, source_target_pairs={{0,1},{1,0},{2,3},{3,2},{4,5},{5,4},{6,7},{7,6},{8,9},{9,8},{10,11... | collective-permute-start | bytes 786440 | tf_op jit(solution)/shard_map/ppermute | solution.py:454
  19.4 13.0 %collective-permute-start.9 = (f32[168,128]{1,0:T(8,128)S(1)}, f32[168,128]{1,0:T(8,128)S(1)}, u32[]{:S(2)}, u32[]{:S(2)}) collective-permute-start(f32[168,128]{1,0:T(8,128)S(1)} %add.109), channel_id=1, source_target_pairs={{4,8},{8,4},{5,9},{9,5},{6,10},{10,6},{7,11},{11,7},{20,24},{24,20... | collective-permute-start | bytes 258056 | tf_op jit(solution)/shard_map/ppermute | solution.py:462
  21.0 10.7 %collective-permute-start.5 = (f32[128,384]{1,0:T(8,128)S(1)}, f32[128,384]{1,0:T(8,128)S(1)}, u32[]{:S(2)}, u32[]{:S(2)}) collective-permute-start(f32[128,384]{1,0:T(8,128)S(1)} %bitcast_add_fusion), channel_id=1, source_target_pairs={{0,4},{12,8},{1,5},{13,9},{2,6},{14,10},{3,7},{15,11},{16,20},{28,... | collective-permute-start | bytes 589832 | tf_op jit(solution)/shard_map/ppermute | solution.py:470
  27.6 14.5 %collective-permute-start.15 = (f32[128,640]{1,0:T(8,128)S(1)}, f32[128,640]{1,0:T(8,128)S(1)}, u32[]{:S(2)}, u32[]{:S(2)}) collective-permute-start(f32[128,640]{1,0:T(8,128)S(1)} %dynamic-slice_add_fusion.1), channel_id=1, source_target_pairs={{0,4},{12,8},{1,5},{13,9},{2,6},{14,10},{3,7},{15,11},{16,20},{28,... | collective-permute-start | bytes 983048 | tf_op jit(solution)/shard_map/ppermute | solution.py:470
  31.7 11.1 %collective-permute-start.8 = (f32[128,384]{1,0:T(8,128)S(1)}, f32[128,384]{1,0:T(8,128)S(1)}, u32[]{:S(2)}, u32[]{:S(2)}) collective-permute-start(f32[128,384]{1,0:T(8,128)S(1)} %add.125.refs_1_), channel_id=1, source_target_pairs={{4,8},{8,4},{5,9},{9,5},{6,10},{10,6},{7,11},{11,7},{20,24},{24,20... | collective-permute-start | bytes 589832 | tf_op jit(solution)/shard_map/ppermute | solution.py:483
  32.5 15.8 %collective-permute-start.10 = (f32[128,384]{1,0:T(8,128)S(1)}, f32[128,384]{1,0:T(8,128)S(1)}, u32[]{:S(2)}, u32[]{:S(2)}) collective-permute-start(f32[128,384]{1,0:T(8,128)S(1)} %add.125.refs_1_), channel_id=1, source_target_pairs={{0,1},{1,0},{2,3},{3,2},{4,5},{5,4},{6,7},{7,6},{8,9},{9,8},{10,11... | collective-permute-start | bytes 589832 | tf_op jit(solution)/shard_map/ppermute | solution.py:487
  32.5 22.9 %collective-permute-start.13 = (f32[128,896]{1,0:T(8,128)S(1)}, f32[128,896]{1,0:T(8,128)S(1)}, u32[]{:S(2)}, u32[]{:S(2)}) collective-permute-start(f32[128,896]{1,0:T(8,128)S(1)} %dynamic-slice_add_fusion), channel_id=1, source_target_pairs={{0,4},{12,8},{1,5},{13,9},{2,6},{14,10},{3,7},{15,11},{16,20},{28,... | collective-permute-start | bytes 1376264 | tf_op jit(solution)/shard_map/ppermute | solution.py:470
  42.1 32.6 %copy-start.6 = (bf16[256,384]{1,0:T(8,128)(2,1)}, bf16[256,384]{1,0:T(8,128)(2,1)S(1)}, u32[]{:S(2)}) copy-start(bf16[256,384]{1,0:T(8,128)(2,1)S(1)} %get-tuple-element.46.refs_7_) | copy-start | bytes 589828
  42.2 14.3 %collective-permute-start.16 = (f32[128,640]{1,0:T(8,128)S(1)}, f32[128,640]{1,0:T(8,128)S(1)}, u32[]{:S(2)}, u32[]{:S(2)}) collective-permute-start(f32[128,640]{1,0:T(8,128)S(1)} %add.129.refs_1_), channel_id=1, source_target_pairs={{4,8},{8,4},{5,9},{9,5},{6,10},{10,6},{7,11},{11,7},{20,24},{24,20... | collective-permute-start | bytes 983048 | tf_op jit(solution)/shard_map/ppermute | solution.py:483
  42.9 5.4 %collective-permute-start.11 = (f32[128,384]{1,0:T(8,128)S(1)}, f32[128,384]{1,0:T(8,128)S(1)}, u32[]{:S(2)}, u32[]{:S(2)}) collective-permute-start(f32[128,384]{1,0:T(8,128)S(1)} %collective-permute-done.8.refs_2_), channel_id=1, source_target_pairs={{0,1},{1,0},{2,3},{3,2},{4,5},{5,4},{6,7},{7,6},{8,9},{9,8},{10,11... | collective-permute-start | bytes 589832 | tf_op jit(solution)/shard_map/ppermute | solution.py:487
  44.1 12.2 %collective-permute-start.3 = (f32[64,1024]{1,0:T(8,128)S(1)}, f32[64,1024]{1,0:T(8,128)S(1)}, u32[]{:S(2)}, u32[]{:S(2)}) collective-permute-start(f32[64,1024]{1,0:T(8,128)S(1)} %dynamic-slice_add_fusion.2), channel_id=1, source_target_pairs={{0,4},{12,8},{1,5},{13,9},{2,6},{14,10},{3,7},{15,11},{16,20},{28,... | collective-permute-start | bytes 786440 | tf_op jit(solution)/shard_map/ppermute | solution.py:470
  55.4 29.6 %copy-start.2 = (bf16[1024,384]{1,0:T(8,128)(2,1)}, bf16[1024,384]{1,0:T(8,128)(2,1)S(1)}, u32[]{:S(2)}) copy-start(bf16[1024,384]{1,0:T(8,128)(2,1)S(1)} %get-tuple-element.53.refs_8_) | copy-start | bytes 2359300
  55.5 11.8 %collective-permute-start.14 = (f32[128,896]{1,0:T(8,128)S(1)}, f32[128,896]{1,0:T(8,128)S(1)}, u32[]{:S(2)}, u32[]{:S(2)}) collective-permute-start(f32[128,896]{1,0:T(8,128)S(1)} %add.128.refs_1_), channel_id=1, source_target_pairs={{4,8},{8,4},{5,9},{9,5},{6,10},{10,6},{7,11},{11,7},{20,24},{24,20... | collective-permute-start | bytes 1376264 | tf_op jit(solution)/shard_map/ppermute | solution.py:483
  56.4 1.7 %collective-permute-start.17 = (f32[128,640]{1,0:T(8,128)S(1)}, f32[128,640]{1,0:T(8,128)S(1)}, u32[]{:S(2)}, u32[]{:S(2)}) collective-permute-start(f32[128,640]{1,0:T(8,128)S(1)} %add.129.refs_1_), channel_id=1, source_target_pairs={{0,1},{1,0},{2,3},{3,2},{4,5},{5,4},{6,7},{7,6},{8,9},{9,8},{10,11... | collective-permute-start | bytes 983048 | tf_op jit(solution)/shard_map/ppermute | solution.py:487
  56.5 2.1 %collective-permute-start.18 = (f32[128,640]{1,0:T(8,128)S(1)}, f32[128,640]{1,0:T(8,128)S(1)}, u32[]{:S(2)}, u32[]{:S(2)}) collective-permute-start(f32[128,640]{1,0:T(8,128)S(1)} %collective-permute-done.16.refs_2_), channel_id=1, source_target_pairs={{0,1},{1,0},{2,3},{3,2},{4,5},{5,4},{6,7},{7,6},{8,9},{9,8},{10,11... | collective-permute-start | bytes 983048 | tf_op jit(solution)/shard_map/ppermute | solution.py:487
  57.0 17.7 %collective-permute-start.19 = (f32[128,896]{1,0:T(8,128)S(1)}, f32[128,896]{1,0:T(8,128)S(1)}, u32[]{:S(2)}, u32[]{:S(2)}) collective-permute-start(f32[128,896]{1,0:T(8,128)S(1)} %add.128.refs_1_), channel_id=1, source_target_pairs={{0,1},{1,0},{2,3},{3,2},{4,5},{5,4},{6,7},{7,6},{8,9},{9,8},{10,11... | collective-permute-start | bytes 1376264 | tf_op jit(solution)/shard_map/ppermute | solution.py:487
  67.3 19.3 %copy-start.4 = (f32[256,640]{1,0:T(8,128)}, f32[256,640]{1,0:T(8,128)S(1)}, u32[]{:S(2)}) copy-start(f32[256,640]{1,0:T(8,128)S(1)} %get-tuple-element.62.refs_13_) | copy-start | bytes 1966084
  67.3 7.4 %collective-permute-start.20 = (f32[128,896]{1,0:T(8,128)S(1)}, f32[128,896]{1,0:T(8,128)S(1)}, u32[]{:S(2)}, u32[]{:S(2)}) collective-permute-start(f32[128,896]{1,0:T(8,128)S(1)} %collective-permute-done.14.refs_2_), channel_id=1, source_target_pairs={{0,1},{1,0},{2,3},{3,2},{4,5},{5,4},{6,7},{7,6},{8,9},{9,8},{10,11... | collective-permute-start | bytes 1376264 | tf_op jit(solution)/shard_map/ppermute | solution.py:487
  67.5 19.1 %collective-permute-start.12 = (f32[64,1024]{1,0:T(8,128)S(1)}, f32[64,1024]{1,0:T(8,128)}, u32[]{:S(2)}, u32[]{:S(2)}) collective-permute-start(f32[64,1024]{1,0:T(8,128)S(1)} %add.127.refs_1_), channel_id=1, source_target_pairs={{4,8},{8,4},{5,9},{9,5},{6,10},{10,6},{7,11},{11,7},{20,24},{24,20... | collective-permute-start | bytes 786440 | tf_op jit(solution)/shard_map/ppermute | solution.py:483
  68.8 18.2 %collective-permute-start.23 = (bf16[128,1024]{1,0:T(8,128)(2,1)}, bf16[128,1024]{1,0:T(8,128)(2,1)}, u32[]{:S(2)}, u32[]{:S(2)}) collective-permute-start(bf16[128,1024]{1,0:T(8,128)(2,1)} %bitcast.7.refs_0_), channel_id=1, source_target_pairs={{0,4},{12,8},{1,5},{13,9},{2,6},{14,10},{3,7},{15,11},{16,20},{28,... | collective-permute-start | bytes 786440 | tf_op jit(solution)/shard_map/ppermute | solution.py:493
  74.6 15.2 %collective-permute-start.21 = (f32[64,1024]{1,0:T(8,128)S(1)}, f32[64,1024]{1,0:T(8,128)}, u32[]{:S(2)}, u32[]{:S(2)}) collective-permute-start(f32[64,1024]{1,0:T(8,128)S(1)} %add.127.refs_1_), channel_id=1, source_target_pairs={{0,1},{1,0},{2,3},{3,2},{4,5},{5,4},{6,7},{7,6},{8,9},{9,8},{10,11... | collective-permute-start | bytes 786440 | tf_op jit(solution)/shard_map/ppermute | solution.py:487
  85.0 0.9 copy-start
  86.0 0.6 copy-start.9
  86.6 3.2 %collective-permute-start.22 = (f32[64,1024]{1,0:T(8,128)}, f32[64,1024]{1,0:T(8,128)}, u32[]{:S(2)}, u32[]{:S(2)}) collective-permute-start(f32[64,1024]{1,0:T(8,128)} %collective-permute-done.12.refs_2_), channel_id=1, source_target_pairs={{0,1},{1,0},{2,3},{3,2},{4,5},{5,4},{6,7},{7,6},{8,9},{9,8},{10,11... | collective-permute-start | bytes 786440 | tf_op jit(solution)/shard_map/ppermute | solution.py:487
  87.1 21.9 %collective-permute-start.24 = (bf16[128,1024]{1,0:T(8,128)(2,1)}, bf16[128,1024]{1,0:T(8,128)(2,1)}, u32[]{:S(2)}, u32[]{:S(2)}) collective-permute-start(bf16[128,1024]{1,0:T(8,128)(2,1)} %bitcast.7.refs_0_), channel_id=1, source_target_pairs={{4,8},{8,4},{5,9},{9,5},{6,10},{10,6},{7,11},{11,7},{20,24},{24,20... | collective-permute-start | bytes 786440 | tf_op jit(solution)/shard_map/ppermute | solution.py:496
  88.4 20.6 %collective-permute-start.25 = (bf16[128,1024]{1,0:T(8,128)(2,1)}, bf16[128,1024]{1,0:T(8,128)(2,1)}, u32[]{:S(2)}, u32[]{:S(2)}) collective-permute-start(bf16[128,1024]{1,0:T(8,128)(2,1)} %collective-permute-done.23.refs_1_), channel_id=1, source_target_pairs={{4,8},{8,4},{5,9},{9,5},{6,10},{10,6},{7,11},{11,7},{20,24},{24,20... | collective-permute-start | bytes 786440 | tf_op jit(solution)/shard_map/ppermute | solution.py:496
  89.8 1.2 copy-start.1
  91.0 1.1 copy-start.3
  92.1 1.1 copy-start.5
  93.2 0.9 copy-start.7
  94.2 0.7 copy-start.10
  108.4 0.6 copy-start.8
  111.3 5.8 %collective-permute-start.26 = (f32[8,512]{1,0:T(8,128)}, f32[8,512]{1,0:T(8,128)S(1)}, u32[]{:S(2)}, u32[]{:S(2)}) collective-permute-start(f32[8,512]{1,0:T(8,128)} %score.1), channel_id=1, source_target_pairs={{4,0},{8,12},{5,1},{9,13},{6,2},{10,14},{7,3},{11,15},{20,16},{24,... | collective-permute-start | bytes 49160 | tf_op jit(solution)/shard_map/ppermute | solution.py:431
  117.8 3.6 %collective-permute-start.27 = (f32[1,512]{1,0:T(1,128)S(1)}, f32[1,512]{1,0:T(1,128)S(1)}, u32[]{:S(2)}, u32[]{:S(2)}) collective-permute-start(f32[1,512]{1,0:T(1,128)S(1)} %broadcast_select_fusion), channel_id=1, source_target_pairs={{0,2},{2,0},{1,3},{3,1},{4,6},{6,4},{5,7},{7,5},{8,10},{10,8},{9,1... | collective-permute-start | bytes 6152 | tf_op jit(solution)/shard_map/ppermute | solution.py:504

commit v2 on v1

--- a/solution.py
+++ b/solution.py
@@ -383,7 +383,7 @@
             pltpu.SemaphoreType.DMA((len(earlier) + 2,)),
         ]
         + [pltpu.VMEM(x.shape, x.dtype) for x in earlier],
-        compiler_params=pltpu.CompilerParams(vmem_limit_bytes=40 << 20),
+        compiler_params=pltpu.CompilerParams(vmem_limit_bytes=(60 if last else 40) << 20),
         cost_estimate=pl.CostEstimate(flops=1_200_000_000, bytes_accessed=4_000_000, transcendentals=0),
         name="panel%d" % c,
     )(*inputs, *earlier)

time: 123 us -> 120 us (0.976)
  local copies, waits for them, and re-layouts: 11.2 us -> 8.24 us
  starting transfers between devices: 40.4 us -> 39 us
  waiting for transfers between devices: 9.95 us -> 11.2 us
    unnamed x22 -> x36, local copies, waits for them, and re-layouts: 7.24 us -> 4.28 us
  transfers between devices with their start and end apart: 28 -> 28, of which waited for: 6 -> 6; matrix products, arithmetic and copies ran while one was open for 7% -> 8% of each run, Pallas kernels for 35% -> 36%
where the time goes in v2:
time: 120 us; the launch traced here: 119 us
  Pallas kernels  52.5 us (44%)
  starting transfers between devices  39 us (32%)
  waiting for transfers between devices  11.2 us (9%)
  local copies, waits for them, and re-layouts  8.24 us (7%)
  other arithmetic  7.06 us (6%)
  between operations  1.23 us (1%)
    pallas_call x5, Pallas kernels, panel(): pl.pallas_call(functools.partial(panel_kernel, c, size, seqs, padded), in...  43.2 us
    ppermute x4, starting transfers between devices, inwards(): x = x + after(lax.ppermute(x, 'dp', step), *gate)  17 us
    pallas_call x1, Pallas kernels, project(): pl.pallas_call(functools.partial(project_kernel, steps, seqs), grid=(step...  7.04 us
    ppermute x1, starting transfers between devices, body(): near = near[:1] + [lax.ppermute(x, 'dp', step) for x in near]  6 us
    ppermute x1, waiting for transfers between devices, from_middle(): got = lax.ppermute(x, 'dp', [(s + 1, s), (n - 2 - s, n - 1 - s)])  5.75 us
    ppermute x2, starting transfers between devices, body(): first = first + lax.ppermute(first, 'dp', step)  5.54 us
    unnamed x36, local copies, waits for them, and re-layouts  4.28 us
    dynamic_slice x4, local copies, waits for them, and re-layouts, over_rep(): other = lax.dynamic_slice(array, (top + (1 - rep) * half, 0), (half, wide))  3.97 us
  transfers between devices with their start and end apart: 28, of which 6 were waited for; matrix products, arithmetic and copies ran while one was open for 8% of the time, Pallas kernels for 36%

profile of v2, /device:TPU:0, one launch (start us, length us, event | category | flops | bytes accessed | tf_op | source)
XLA Modules:
  0.0 119.3 jit_solution(12843701605513269503)
XLA Ops:
  0.7 0.6 pad_add_fusion.place_ref
  1.3 7.0 %project.1 = f32[168,128]{1,0:T(8,128)} custom-call(s32[3]{0:T(128)} %pad_add_fusion.place_ref, bf16[1,1,512,4096]{3,2,1,0:T(8,128)(2,1)} %act_ref.1, bf16[1,1,512,4096]{3,2,1,0:T(8,128)(2,1)} %grad_ref.1, bf16[1,32,4096]{2,1,0:T(8,128)(2,1)} %pin_ref.1, bf16[1,32,4096]{2,1,0:T(8,128)(2,1)} %pout_ref.1, f32[1,1,1024,1024]{3,2,1,0:T(8,128)} %prior_ref.1), custom_call_target="tpu_custom_call" | custom-call | tf_op jit(solution)/shard_map/project/pallas_call | solution.py:110
  8.3 0.5 collective-permute-start
  8.8 0.9 dynamic-slice_bitcast_fusion
  9.9 0.9 add.103
  10.8 4.9 %collective-permute-start.2 = (f32[168,128]{1,0:T(8,128)S(1)}, f32[168,128]{1,0:T(8,128)S(1)}, u32[]{:S(2)}, u32[]{:S(2)}) collective-permute-start(f32[168,128]{1,0:T(8,128)S(1)} %add.103), channel_id=1, source_target_pairs={{0,4},{12,8},{1,5},{13,9},{2,6},{14,10},{3,7},{15,11},{16,20},{28,... | collective-permute-start | bytes 258056 | tf_op jit(solution)/shard_map/ppermute | solution.py:462
  15.7 1.1 constant_dynamic-slice_fusion.2
  16.8 1.0 constant_dynamic-slice_fusion.3
  17.8 0.6 collective-permute-start.6
  18.4 1.0 constant_dynamic-slice_fusion.4
  19.5 0.7 collective-permute-start.9
  20.1 1.0 bitcast_add_fusion
  21.1 5.5 %collective-permute-start.5 = (f32[128,384]{1,0:T(8,128)S(1)}, f32[128,384]{1,0:T(8,128)S(1)}, u32[]{:S(2)}, u32[]{:S(2)}) collective-permute-start(f32[128,384]{1,0:T(8,128)S(1)} %bitcast_add_fusion), channel_id=1, source_target_pairs={{0,4},{12,8},{1,5},{13,9},{2,6},{14,10},{3,7},{15,11},{16,20},{28,... | collective-permute-start | bytes 589832 | tf_op jit(solution)/shard_map/ppermute | solution.py:470
  26.6 1.0 dynamic-slice_add_fusion.1
  27.7 1.3 %collective-permute-start.15 = (f32[128,640]{1,0:T(8,128)S(1)}, f32[128,640]{1,0:T(8,128)S(1)}, u32[]{:S(2)}, u32[]{:S(2)}) collective-permute-start(f32[128,640]{1,0:T(8,128)S(1)} %dynamic-slice_add_fusion.1), channel_id=1, source_target_pairs={{0,4},{12,8},{1,5},{13,9},{2,6},{14,10},{3,7},{15,11},{16,20},{28,... | collective-permute-start | bytes 983048 | tf_op jit(solution)/shard_map/ppermute | solution.py:470
  29.0 1.1 dynamic-slice_add_fusion
  30.1 1.7 %collective-permute-done.5 = f32[128,384]{1,0:T(8,128)S(1)} collective-permute-done((f32[128,384]{1,0:T(8,128)S(1)}, f32[128,384]{1,0:T(8,128)S(1)}, u32[]{:S(2)}, u32[]{:S(2)}) %collective-permute-start.5) | collective-permute-done | bytes 196640 | tf_op jit(solution)/shard_map/ppermute | solution.py:470
  31.8 0.7 collective-permute-start.8
  32.6 6.1 %collective-permute-start.13 = (f32[128,896]{1,0:T(8,128)S(1)}, f32[128,896]{1,0:T(8,128)S(1)}, u32[]{:S(2)}, u32[]{:S(2)}) collective-permute-start(f32[128,896]{1,0:T(8,128)S(1)} %dynamic-slice_add_fusion), channel_id=1, source_target_pairs={{0,4},{12,8},{1,5},{13,9},{2,6},{14,10},{3,7},{15,11},{16,20},{28,... | collective-permute-start | bytes 1376264 | tf_op jit(solution)/shard_map/ppermute | solution.py:470
  38.7 3.5 %panel0.1 = (f32[16,1024]{1,0:T(8,128)S(1)}, f32[8,128]{1,0:T(8,128)S(1)}, bf16[256,384]{1,0:T(8,128)(2,1)S(1)}, f32[128,128]{1,0:T(8,128)S(1)}) custom-call(f32[168,128]{1,0:T(8,128)S(1)} %add.126.refs_0_), custom_call_target="tpu_custom_call" | custom-call | flops 1200000000 | bytes 4000000 | tf_op jit(solution)/shard_map/panel0/pallas_call | solution.py:374
  42.3 0.7 collective-permute-start.16
  43.2 1.0 dynamic-slice_add_fusion.2
  44.2 4.1 %collective-permute-start.3 = (f32[64,1024]{1,0:T(8,128)S(1)}, f32[64,1024]{1,0:T(8,128)S(1)}, u32[]{:S(2)}, u32[]{:S(2)}) collective-permute-start(f32[64,1024]{1,0:T(8,128)S(1)} %dynamic-slice_add_fusion.2), channel_id=1, source_target_pairs={{0,4},{12,8},{1,5},{13,9},{2,6},{14,10},{3,7},{15,11},{16,20},{28,... | collective-permute-start | bytes 786440 | tf_op jit(solution)/shard_map/ppermute | solution.py:470
  48.3 7.2 %panel1.1 = (f32[8,384]{1,0:T(8,128)S(1)}, bf16[1024,384]{1,0:T(8,128)(2,1)S(1)}, f32[256,384]{1,0:T(8,128)S(1)}) custom-call(s32[1]{0:T(128)} %bitcast.1.refs_0_, f32[128,384]{1,0:T(8,128)S(1)} %add.125.refs_1_, f32[128,384]{1,0:T(8,128)S(1)} %collective-permute-done.8.refs_2_, f32[128,384]{1,0:T(8,128)S(1)} %collective-permute-done.10.refs_3_, ...), custom_call_target="tpu_custom_call" | custom-call | flops 1200000000 | bytes 4000000 | tf_op jit(solution)/shard_map/panel1/pallas_call | solution.py:374
  55.6 1.0 collective-permute-start.14
  56.8 0.5 collective-permute-start.18
  57.3 1.0 collective-permute-done.17.refs_3_
  58.4 0.5 collective-permute-done.18.refs_4_
  58.8 8.7 %panel2.1 = (f32[8,640]{1,0:T(8,128)S(1)}, bf16[1536,384]{1,0:T(8,128)(2,1)S(1)}, f32[256,640]{1,0:T(8,128)S(1)}) custom-call(s32[1]{0:T(128)} %bitcast.1.refs_0_, f32[128,640]{1,0:T(8,128)S(1)} %add.129.refs_1_, f32[128,640]{1,0:T(8,128)S(1)} %collective-permute-done.16.refs_2_, f32[128,640]{1,0:T(8,128)S(1)} %collective-permute-done.17.refs_3_, ...), custom_call_target="tpu_custom_call" | custom-call | flops 1200000000 | bytes 4000000 | tf_op jit(solution)/shard_map/panel2/pallas_call | solution.py:374
  67.8 0.7 collective-permute-start.12
  68.5 6.0 %collective-permute-start.23 = (bf16[128,1024]{1,0:T(8,128)(2,1)S(1)}, bf16[128,1024]{1,0:T(8,128)(2,1)S(1)}, u32[]{:S(2)}, u32[]{:S(2)}) collective-permute-start(bf16[128,1024]{1,0:T(8,128)(2,1)S(1)} %bitcast.17), channel_id=1, source_target_pairs={{0,4},{12,8},{1,5},{13,9},{2,6},{14,10},{3,7},{15,11},{16,20},{28,... | collective-permute-start | bytes 786440 | tf_op jit(solution)/shard_map/ppermute | solution.py:493
  74.6 10.3 %panel3.1 = (f32[8,896]{1,0:T(8,128)S(1)}, bf16[2048,384]{1,0:T(8,128)(2,1)S(1)}, f32[256,896]{1,0:T(8,128)S(1)}) custom-call(s32[1]{0:T(128)} %bitcast.1.refs_0_, f32[128,896]{1,0:T(8,128)S(1)} %add.128.refs_1_, f32[128,896]{1,0:T(8,128)S(1)} %collective-permute-done.14.refs_2_, f32[128,896]{1,0:T(8,128)S(1)} %collective-permute-done.19.refs_3_, ...), custom_call_target="tpu_custom_call" | custom-call | flops 1200000000 | bytes 4000000 | tf_op jit(solution)/shard_map/panel3/pallas_call | solution.py:374
  85.0 1.2 copy-done
  86.1 0.9 copy-done.2
  87.1 0.6 copy-done.9
  87.7 0.5 collective-permute-start.22
  88.2 0.7 collective-permute-start.24
  88.9 0.9 collective-permute-start.25
  89.9 0.7 copy-done.12
  90.7 13.6 %panel4.1.solved_ref = f32[8,1024]{1,0:T(8,128)} custom-call(s32[1]{0:T(128)} %bitcast.1.refs_0_, f32[64,1024]{1,0:T(8,128)} %copy-done.10, f32[64,1024]{1,0:T(8,128)} %copy-done.11, f32[64,1024]{1,0:T(8,128)} %copy-done.12, f32[64,1024]{1,0:T(8,128)} %copy-done.13, f32[16,1024]{1,0:T(8,128)} %copy-done.7, f32[8,896]{1,0:T(8,128)} %copy-done.9, ...), custom_call_target="tpu_custom_call" | custom-call | flops 1200000000 | bytes 4000000 | tf_op jit(solution)/shard_map/panel4/pallas_call | solution.py:374
  104.3 0.7 copy-done.16
  105.1 2.3 %score.1 = f32[8,512]{1,0:T(8,128)} custom-call(s32[1]{0:T(128)} %bitcast.side_ref, f32[8,1024]{1,0:T(8,128)} %panel4.1.solved_ref, bf16[128,1024]{1,0:T(8,128)(2,1)} %bitcast.16, bf16[128,1024]{1,0:T(8,128)(2,1)} %copy-done.15, bf16[128,1024]{1,0:T(8,128)(2,1)} %copy-done.16, bf16[128,1024]{1,0:T(8,128)(2,1)} %copy-done.17), custom_call_target="tpu_custom_call" | custom-call | tf_op jit(solution)/shard_map/score/pallas_call | solution.py:409
  107.4 1.3 %collective-permute-start.26 = (f32[8,512]{1,0:T(8,128)}, f32[8,512]{1,0:T(8,128)S(1)}, u32[]{:S(2)}, u32[]{:S(2)}) collective-permute-start(f32[8,512]{1,0:T(8,128)} %score.1), channel_id=1, source_target_pairs={{4,0},{8,12},{5,1},{9,13},{6,2},{10,14},{7,3},{11,15},{20,16},{24,... | collective-permute-start | bytes 49160 | tf_op jit(solution)/shard_map/ppermute | solution.py:431
  108.7 5.8 %collective-permute-done.26 = f32[8,512]{1,0:T(8,128)S(1)} collective-permute-done((f32[8,512]{1,0:T(8,128)}, f32[8,512]{1,0:T(8,128)S(1)}, u32[]{:S(2)}, u32[]{:S(2)}) %collective-permute-start.26) | collective-permute-done | bytes 16416 | tf_op jit(solution)/shard_map/ppermute | solution.py:431
  114.4 0.7 broadcast_select_fusion
  115.1 1.5 %collective-permute-start.27 = (f32[1,512]{1,0:T(1,128)S(1)}, f32[1,512]{1,0:T(1,128)S(1)}, u32[]{:S(2)}, u32[]{:S(2)}) collective-permute-start(f32[1,512]{1,0:T(1,128)S(1)} %broadcast_select_fusion), channel_id=1, source_target_pairs={{0,2},{2,0},{1,3},{3,1},{4,6},{6,4},{5,7},{7,5},{8,10},{10,8},{9,1... | collective-permute-start | bytes 6152 | tf_op jit(solution)/shard_map/ppermute | solution.py:504
  116.6 2.1 %collective-permute-done.27 = f32[1,512]{1,0:T(1,128)S(1)} collective-permute-done((f32[1,512]{1,0:T(1,128)S(1)}, f32[1,512]{1,0:T(1,128)S(1)}, u32[]{:S(2)}, u32[]{:S(2)}) %collective-permute-start.27) | collective-permute-done | bytes 2080 | tf_op jit(solution)/shard_map/ppermute | solution.py:504
  118.7 0.6 add.131
  (69 shorter events, 1.6 us)
Async XLA Ops:
  8.3 1.6 %collective-permute-start = (f32[168,128]{1,0:T(8,128)}, f32[168,128]{1,0:T(8,128)S(1)}, u32[]{:S(2)}, u32[]{:S(2)}) collective-permute-start(f32[168,128]{1,0:T(8,128)} %project.1), channel_id=1, source_target_pairs={{0,1},{1,0},{2,3},{3,2},{4,5},{5,4},{6,7},{7,6},{8,9},{9,8},{10,11... | collective-permute-start | bytes 258056 | tf_op jit(solution)/shard_map/ppermute | solution.py:459
  9.7 10.4 %collective-permute-start.4 = (f32[128,384]{1,0:T(8,128)S(1)}, f32[128,384]{1,0:T(8,128)S(1)}, u32[]{:S(2)}, u32[]{:S(2)}) collective-permute-start(f32[128,384]{1,0:T(8,128)S(1)} %dynamic-slice_bitcast_fusion), channel_id=1, source_target_pairs={{0,1},{1,0},{2,3},{3,2},{4,5},{5,4},{6,7},{7,6},{8,9},{9,8},{10,11... | collective-permute-start | bytes 589832 | tf_op jit(solution)/shard_map/ppermute | solution.py:454
  10.8 8.6 %collective-permute-start.2 = (f32[168,128]{1,0:T(8,128)S(1)}, f32[168,128]{1,0:T(8,128)S(1)}, u32[]{:S(2)}, u32[]{:S(2)}) collective-permute-start(f32[168,128]{1,0:T(8,128)S(1)} %add.103), channel_id=1, source_target_pairs={{0,4},{12,8},{1,5},{13,9},{2,6},{14,10},{3,7},{15,11},{16,20},{28,... | collective-permute-start | bytes 258056 | tf_op jit(solution)/shard_map/ppermute | solution.py:462
  16.7 12.2 %collective-permute-start.7 = (f32[128,896]{1,0:T(8,128)S(1)}, f32[128,896]{1,0:T(8,128)S(1)}, u32[]{:S(2)}, u32[]{:S(2)}) collective-permute-start(f32[128,896]{1,0:T(8,128)S(1)} %constant_dynamic-slice_fusion.2), channel_id=1, source_target_pairs={{0,1},{1,0},{2,3},{3,2},{4,5},{5,4},{6,7},{7,6},{8,9},{9,8},{10,11... | collective-permute-start | bytes 1376264 | tf_op jit(solution)/shard_map/ppermute | solution.py:454
  17.8 8.8 %collective-permute-start.6 = (f32[128,640]{1,0:T(8,128)S(1)}, f32[128,640]{1,0:T(8,128)S(1)}, u32[]{:S(2)}, u32[]{:S(2)}) collective-permute-start(f32[128,640]{1,0:T(8,128)S(1)} %constant_dynamic-slice_fusion.3), channel_id=1, source_target_pairs={{0,1},{1,0},{2,3},{3,2},{4,5},{5,4},{6,7},{7,6},{8,9},{9,8},{10,11... | collective-permute-start | bytes 983048 | tf_op jit(solution)/shard_map/ppermute | solution.py:454
  19.3 23.9 %collective-permute-start.1 = (f32[64,1024]{1,0:T(8,128)S(1)}, f32[64,1024]{1,0:T(8,128)S(1)}, u32[]{:S(2)}, u32[]{:S(2)}) collective-permute-start(f32[64,1024]{1,0:T(8,128)S(1)} %constant_dynamic-slice_fusion.4), channel_id=1, source_target_pairs={{0,1},{1,0},{2,3},{3,2},{4,5},{5,4},{6,7},{7,6},{8,9},{9,8},{10,11... | collective-permute-start | bytes 786440 | tf_op jit(solution)/shard_map/ppermute | solution.py:454
  19.5 13.1 %collective-permute-start.9 = (f32[168,128]{1,0:T(8,128)S(1)}, f32[168,128]{1,0:T(8,128)S(1)}, u32[]{:S(2)}, u32[]{:S(2)}) collective-permute-start(f32[168,128]{1,0:T(8,128)S(1)} %add.109), channel_id=1, source_target_pairs={{4,8},{8,4},{5,9},{9,5},{6,10},{10,6},{7,11},{11,7},{20,24},{24,20... | collective-permute-start | bytes 258056 | tf_op jit(solution)/shard_map/ppermute | solution.py:462
  21.1 10.7 %collective-permute-start.5 = (f32[128,384]{1,0:T(8,128)S(1)}, f32[128,384]{1,0:T(8,128)S(1)}, u32[]{:S(2)}, u32[]{:S(2)}) collective-permute-start(f32[128,384]{1,0:T(8,128)S(1)} %bitcast_add_fusion), channel_id=1, source_target_pairs={{0,4},{12,8},{1,5},{13,9},{2,6},{14,10},{3,7},{15,11},{16,20},{28,... | collective-permute-start | bytes 589832 | tf_op jit(solution)/shard_map/ppermute | solution.py:470
  27.7 14.6 %collective-permute-start.15 = (f32[128,640]{1,0:T(8,128)S(1)}, f32[128,640]{1,0:T(8,128)S(1)}, u32[]{:S(2)}, u32[]{:S(2)}) collective-permute-start(f32[128,640]{1,0:T(8,128)S(1)} %dynamic-slice_add_fusion.1), channel_id=1, source_target_pairs={{0,4},{12,8},{1,5},{13,9},{2,6},{14,10},{3,7},{15,11},{16,20},{28,... | collective-permute-start | bytes 983048 | tf_op jit(solution)/shard_map/ppermute | solution.py:470
  31.8 11.1 %collective-permute-start.8 = (f32[128,384]{1,0:T(8,128)S(1)}, f32[128,384]{1,0:T(8,128)S(1)}, u32[]{:S(2)}, u32[]{:S(2)}) collective-permute-start(f32[128,384]{1,0:T(8,128)S(1)} %add.125.refs_1_), channel_id=1, source_target_pairs={{4,8},{8,4},{5,9},{9,5},{6,10},{10,6},{7,11},{11,7},{20,24},{24,20... | collective-permute-start | bytes 589832 | tf_op jit(solution)/shard_map/ppermute | solution.py:483
  32.5 15.8 %collective-permute-start.10 = (f32[128,384]{1,0:T(8,128)S(1)}, f32[128,384]{1,0:T(8,128)S(1)}, u32[]{:S(2)}, u32[]{:S(2)}) collective-permute-start(f32[128,384]{1,0:T(8,128)S(1)} %add.125.refs_1_), channel_id=1, source_target_pairs={{0,1},{1,0},{2,3},{3,2},{4,5},{5,4},{6,7},{7,6},{8,9},{9,8},{10,11... | collective-permute-start | bytes 589832 | tf_op jit(solution)/shard_map/ppermute | solution.py:487
  32.6 22.9 %collective-permute-start.13 = (f32[128,896]{1,0:T(8,128)S(1)}, f32[128,896]{1,0:T(8,128)S(1)}, u32[]{:S(2)}, u32[]{:S(2)}) collective-permute-start(f32[128,896]{1,0:T(8,128)S(1)} %dynamic-slice_add_fusion), channel_id=1, source_target_pairs={{0,4},{12,8},{1,5},{13,9},{2,6},{14,10},{3,7},{15,11},{16,20},{28,... | collective-permute-start | bytes 1376264 | tf_op jit(solution)/shard_map/ppermute | solution.py:470
  42.2 25.4 %copy-start.8 = (f32[128,128]{1,0:T(8,128)}, f32[128,128]{1,0:T(8,128)S(1)}, u32[]{:S(2)}) copy-start(f32[128,128]{1,0:T(8,128)S(1)} %get-tuple-element.60.refs_11_) | copy-start | bytes 196612
  42.2 32.4 %copy-start.6 = (bf16[256,384]{1,0:T(8,128)(2,1)}, bf16[256,384]{1,0:T(8,128)(2,1)S(1)}, u32[]{:S(2)}) copy-start(bf16[256,384]{1,0:T(8,128)(2,1)S(1)} %get-tuple-element.46.refs_7_) | copy-start | bytes 589828
  42.2 32.4 %copy-start.7 = (f32[16,1024]{1,0:T(8,128)}, f32[16,1024]{1,0:T(8,128)S(1)}, u32[]{:S(2)}) copy-start(f32[16,1024]{1,0:T(8,128)S(1)} %get-tuple-element.43.refs_5_) | copy-start | bytes 196612
  42.3 14.5 %collective-permute-start.16 = (f32[128,640]{1,0:T(8,128)S(1)}, f32[128,640]{1,0:T(8,128)S(1)}, u32[]{:S(2)}, u32[]{:S(2)}) collective-permute-start(f32[128,640]{1,0:T(8,128)S(1)} %add.129.refs_1_), channel_id=1, source_target_pairs={{4,8},{8,4},{5,9},{9,5},{6,10},{10,6},{7,11},{11,7},{20,24},{24,20... | collective-permute-start | bytes 983048 | tf_op jit(solution)/shard_map/ppermute | solution.py:483
  43.0 5.4 %collective-permute-start.11 = (f32[128,384]{1,0:T(8,128)S(1)}, f32[128,384]{1,0:T(8,128)S(1)}, u32[]{:S(2)}, u32[]{:S(2)}) collective-permute-start(f32[128,384]{1,0:T(8,128)S(1)} %collective-permute-done.8.refs_2_), channel_id=1, source_target_pairs={{0,1},{1,0},{2,3},{3,2},{4,5},{5,4},{6,7},{7,6},{8,9},{9,8},{10,11... | collective-permute-start | bytes 589832 | tf_op jit(solution)/shard_map/ppermute | solution.py:487
  44.2 12.4 %collective-permute-start.3 = (f32[64,1024]{1,0:T(8,128)S(1)}, f32[64,1024]{1,0:T(8,128)S(1)}, u32[]{:S(2)}, u32[]{:S(2)}) collective-permute-start(f32[64,1024]{1,0:T(8,128)S(1)} %dynamic-slice_add_fusion.2), channel_id=1, source_target_pairs={{0,4},{12,8},{1,5},{13,9},{2,6},{14,10},{3,7},{15,11},{16,20},{28,... | collective-permute-start | bytes 786440 | tf_op jit(solution)/shard_map/ppermute | solution.py:470
  55.5 3.3 %copy-start.5 = (f32[256,384]{1,0:T(8,128)}, f32[256,384]{1,0:T(8,128)S(1)}, u32[]{:S(2)}) copy-start(f32[256,384]{1,0:T(8,128)S(1)} %get-tuple-element.61.refs_12_) | copy-start | bytes 1179652
  55.5 29.4 %copy-start.3 = (bf16[1024,384]{1,0:T(8,128)(2,1)}, bf16[1024,384]{1,0:T(8,128)(2,1)S(1)}, u32[]{:S(2)}) copy-start(bf16[1024,384]{1,0:T(8,128)(2,1)S(1)} %get-tuple-element.53.refs_8_) | copy-start | bytes 2359300
  55.5 12.9 %copy-start.14 = (bf16[1,1,128,1024]{3,2,1,0:T(8,128)(2,1)S(1)}, bf16[1,1,128,1024]{3,2,1,0:T(8,128)(2,1)}, u32[]{:S(2)}) copy-start(bf16[1,1,128,1024]{3,2,1,0:T(8,128)(2,1)} %param.13) | copy-start | bytes 786436
  55.6 12.0 %collective-permute-start.14 = (f32[128,896]{1,0:T(8,128)S(1)}, f32[128,896]{1,0:T(8,128)S(1)}, u32[]{:S(2)}, u32[]{:S(2)}) collective-permute-start(f32[128,896]{1,0:T(8,128)S(1)} %add.128.refs_1_), channel_id=1, source_target_pairs={{4,8},{8,4},{5,9},{9,5},{6,10},{10,6},{7,11},{11,7},{20,24},{24,20... | collective-permute-start | bytes 1376264 | tf_op jit(solution)/shard_map/ppermute | solution.py:483
  56.7 28.3 %copy-start.10 = (f32[64,1024]{1,0:T(8,128)}, f32[64,1024]{1,0:T(8,128)S(1)}, u32[]{:S(2)}) copy-start(f32[64,1024]{1,0:T(8,128)S(1)} %add.127.refs_1_) | copy-start | bytes 786436
  56.7 1.7 %collective-permute-start.17 = (f32[128,640]{1,0:T(8,128)S(1)}, f32[128,640]{1,0:T(8,128)S(1)}, u32[]{:S(2)}, u32[]{:S(2)}) collective-permute-start(f32[128,640]{1,0:T(8,128)S(1)} %add.129.refs_1_), channel_id=1, source_target_pairs={{0,1},{1,0},{2,3},{3,2},{4,5},{5,4},{6,7},{7,6},{8,9},{9,8},{10,11... | collective-permute-start | bytes 983048 | tf_op jit(solution)/shard_map/ppermute | solution.py:487
  56.8 2.1 %collective-permute-start.18 = (f32[128,640]{1,0:T(8,128)S(1)}, f32[128,640]{1,0:T(8,128)S(1)}, u32[]{:S(2)}, u32[]{:S(2)}) collective-permute-start(f32[128,640]{1,0:T(8,128)S(1)} %collective-permute-done.16.refs_2_), channel_id=1, source_target_pairs={{0,1},{1,0},{2,3},{3,2},{4,5},{5,4},{6,7},{7,6},{8,9},{9,8},{10,11... | collective-permute-start | bytes 983048 | tf_op jit(solution)/shard_map/ppermute | solution.py:487
  57.3 17.3 %collective-permute-start.19 = (f32[128,896]{1,0:T(8,128)S(1)}, f32[128,896]{1,0:T(8,128)S(1)}, u32[]{:S(2)}, u32[]{:S(2)}) collective-permute-start(f32[128,896]{1,0:T(8,128)S(1)} %add.128.refs_1_), channel_id=1, source_target_pairs={{0,1},{1,0},{2,3},{3,2},{4,5},{5,4},{6,7},{7,6},{8,9},{9,8},{10,11... | collective-permute-start | bytes 1376264 | tf_op jit(solution)/shard_map/ppermute | solution.py:487
  67.5 20.1 %copy-start.4 = (f32[256,640]{1,0:T(8,128)}, f32[256,640]{1,0:T(8,128)S(1)}, u32[]{:S(2)}) copy-start(f32[256,640]{1,0:T(8,128)S(1)} %get-tuple-element.62.refs_13_) | copy-start | bytes 1966084
  67.6 22.3 %copy-start.1 = (bf16[1536,384]{1,0:T(8,128)(2,1)}, bf16[1536,384]{1,0:T(8,128)(2,1)S(1)}, u32[]{:S(2)}) copy-start(bf16[1536,384]{1,0:T(8,128)(2,1)S(1)} %get-tuple-element.56.refs_9_) | copy-start | bytes 3538948
  67.6 7.0 %collective-permute-start.20 = (f32[128,896]{1,0:T(8,128)S(1)}, f32[128,896]{1,0:T(8,128)S(1)}, u32[]{:S(2)}, u32[]{:S(2)}) collective-permute-start(f32[128,896]{1,0:T(8,128)S(1)} %collective-permute-done.14.refs_2_), channel_id=1, source_target_pairs={{0,1},{1,0},{2,3},{3,2},{4,5},{5,4},{6,7},{7,6},{8,9},{9,8},{10,11... | collective-permute-start | bytes 1376264 | tf_op jit(solution)/shard_map/ppermute | solution.py:487
  67.8 19.9 %collective-permute-start.12 = (f32[64,1024]{1,0:T(8,128)S(1)}, f32[64,1024]{1,0:T(8,128)S(1)}, u32[]{:S(2)}, u32[]{:S(2)}) collective-permute-start(f32[64,1024]{1,0:T(8,128)S(1)} %add.127.refs_1_), channel_id=1, source_target_pairs={{4,8},{8,4},{5,9},{9,5},{6,10},{10,6},{7,11},{11,7},{20,24},{24,20... | collective-permute-start | bytes 786440 | tf_op jit(solution)/shard_map/ppermute | solution.py:483
  68.5 19.8 %collective-permute-start.23 = (bf16[128,1024]{1,0:T(8,128)(2,1)S(1)}, bf16[128,1024]{1,0:T(8,128)(2,1)S(1)}, u32[]{:S(2)}, u32[]{:S(2)}) collective-permute-start(bf16[128,1024]{1,0:T(8,128)(2,1)S(1)} %bitcast.17), channel_id=1, source_target_pairs={{0,4},{12,8},{1,5},{13,9},{2,6},{14,10},{3,7},{15,11},{16,20},{28,... | collective-permute-start | bytes 786440 | tf_op jit(solution)/shard_map/ppermute | solution.py:493
  74.5 15.4 %collective-permute-start.21 = (f32[64,1024]{1,0:T(8,128)S(1)}, f32[64,1024]{1,0:T(8,128)S(1)}, u32[]{:S(2)}, u32[]{:S(2)}) collective-permute-start(f32[64,1024]{1,0:T(8,128)S(1)} %add.127.refs_1_), channel_id=1, source_target_pairs={{0,1},{1,0},{2,3},{3,2},{4,5},{5,4},{6,7},{7,6},{8,9},{9,8},{10,11... | collective-permute-start | bytes 786440 | tf_op jit(solution)/shard_map/ppermute | solution.py:487
  84.9 1.2 copy-start
  86.1 0.9 copy-start.2
  87.1 0.6 copy-start.9
  87.7 2.2 %copy-start.11 = (f32[64,1024]{1,0:T(8,128)}, f32[64,1024]{1,0:T(8,128)S(1)}, u32[]{:S(2)}) copy-start(f32[64,1024]{1,0:T(8,128)S(1)} %collective-permute-done.12.refs_2_) | copy-start | bytes 786436
  87.7 2.2 %collective-permute-start.22 = (f32[64,1024]{1,0:T(8,128)S(1)}, f32[64,1024]{1,0:T(8,128)S(1)}, u32[]{:S(2)}, u32[]{:S(2)}) collective-permute-start(f32[64,1024]{1,0:T(8,128)S(1)} %collective-permute-done.12.refs_2_), channel_id=1, source_target_pairs={{0,1},{1,0},{2,3},{3,2},{4,5},{5,4},{6,7},{7,6},{8,9},{9,8},{10,11... | collective-permute-start | bytes 786440 | tf_op jit(solution)/shard_map/ppermute | solution.py:487
  88.2 16.1 %copy-start.15 = (bf16[128,1024]{1,0:T(8,128)(2,1)}, bf16[128,1024]{1,0:T(8,128)(2,1)S(1)}, u32[]{:S(2)}) copy-start(bf16[128,1024]{1,0:T(8,128)(2,1)S(1)} %collective-permute-done.23.refs_1_) | copy-start | bytes 786436
  88.2 16.0 %collective-permute-start.24 = (bf16[128,1024]{1,0:T(8,128)(2,1)S(1)}, bf16[128,1024]{1,0:T(8,128)(2,1)S(1)}, u32[]{:S(2)}, u32[]{:S(2)}) collective-permute-start(bf16[128,1024]{1,0:T(8,128)(2,1)S(1)} %bitcast.18), channel_id=1, source_target_pairs={{4,8},{8,4},{5,9},{9,5},{6,10},{10,6},{7,11},{11,7},{20,24},{24,20... | collective-permute-start | bytes 786440 | tf_op jit(solution)/shard_map/ppermute | solution.py:496
  88.9 15.4 %collective-permute-start.25 = (bf16[128,1024]{1,0:T(8,128)(2,1)S(1)}, bf16[128,1024]{1,0:T(8,128)(2,1)S(1)}, u32[]{:S(2)}, u32[]{:S(2)}) collective-permute-start(bf16[128,1024]{1,0:T(8,128)(2,1)S(1)} %collective-permute-done.23.refs_1_), channel_id=1, source_target_pairs={{4,8},{8,4},{5,9},{9,5},{6,10},{10,6},{7,11},{11,7},{20,24},{24,20... | collective-permute-start | bytes 786440 | tf_op jit(solution)/shard_map/ppermute | solution.py:496
  89.9 0.7 copy-start.12
  89.9 0.8 copy-start.13
  104.3 0.7 copy-start.16
  104.3 0.8 copy-start.17
  107.4 7.0 %collective-permute-start.26 = (f32[8,512]{1,0:T(8,128)}, f32[8,512]{1,0:T(8,128)S(1)}, u32[]{:S(2)}, u32[]{:S(2)}) collective-permute-start(f32[8,512]{1,0:T(8,128)} %score.1), channel_id=1, source_target_pairs={{4,0},{8,12},{5,1},{9,13},{6,2},{10,14},{7,3},{11,15},{20,16},{24,... | collective-permute-start | bytes 49160 | tf_op jit(solution)/shard_map/ppermute | solution.py:431
  115.1 3.6 %collective-permute-start.27 = (f32[1,512]{1,0:T(1,128)S(1)}, f32[1,512]{1,0:T(1,128)S(1)}, u32[]{:S(2)}, u32[]{:S(2)}) collective-permute-start(f32[1,512]{1,0:T(1,128)S(1)} %broadcast_select_fusion), channel_id=1, source_target_pairs={{0,2},{2,0},{1,3},{3,1},{4,6},{6,4},{5,7},{7,5},{8,10},{10,8},{9,1... | collective-permute-start | bytes 6152 | tf_op jit(solution)/shard_map/ppermute | solution.py:504

commit v3 on v2

--- a/solution.py
+++ b/solution.py
@@ -383,36 +383,36 @@
             pltpu.SemaphoreType.DMA((len(earlier) + 2,)),
         ]
         + [pltpu.VMEM(x.shape, x.dtype) for x in earlier],
-        compiler_params=pltpu.CompilerParams(vmem_limit_bytes=(60 if last else 40) << 20),
+        compiler_params=pltpu.CompilerParams(vmem_limit_bytes=(60 if wide + 2 * NB > size else 40) << 20),
         cost_estimate=pl.CostEstimate(flops=1_200_000_000, bytes_accessed=4_000_000, transcendentals=0),
         name="panel%d" % c,
     )(*inputs, *earlier)
 
 
-def score_kernel(side_ref, solved_ref, *refs):
-    blocks, out_ref = refs[:-1], refs[-1]
+def score_kernel(count, side_ref, solved_ref, *refs):
+    sides, out_ref = refs[:-1], refs[-1]
     rows = solved_ref.shape[0]
-    half = max(len(blocks) // 2, 1)
-    count = blocks[0].shape[0]
+    half = sides[0].shape[0] // count
     solved = jnp.concatenate(split(solved_ref[...]), axis=0)
-    for i, block in enumerate(blocks):
-        terms = by_rows(solved, block[...])
-        low, high = half - 1 - i % half, (half + i % half) if len(blocks) > 1 else 0
-        right_side = side_ref[0] if i < half else 1 - side_ref[0]
-        at = pl.multiple_of((low + right_side * (high - low)) * count, LANES)
-        out_ref[:, pl.ds(at, count)] = terms[0:rows] + terms[rows : 2 * rows] + terms[2 * rows :]
-
-
-def score(side, solved, blocks):
+    for i, side in enumerate(sides):
+        right_side = side_ref[0] if i == 0 else 1 - side_ref[0]
+        for r in range(half):
+            terms = by_rows(solved, side[r * count : (r + 1) * count, :])
+            low, high = half - 1 - r, (half + r if len(sides) > 1 else 0)
+            at = pl.multiple_of((low + right_side * (high - low)) * count, LANES)
+            out_ref[:, pl.ds(at, count)] = terms[0:rows] + terms[rows : 2 * rows] + terms[2 * rows :]
+
+
+def score(count, side, solved, sides):
     vmem = pl.BlockSpec(memory_space=pltpu.VMEM)
-    count = len(blocks) * blocks[0].shape[0]
+    total = len(sides) * sides[0].shape[0]
     return pl.pallas_call(
-        score_kernel,
-        in_specs=[pl.BlockSpec(memory_space=pltpu.SMEM)] + [vmem] * (1 + len(blocks)),
+        functools.partial(score_kernel, count),
+        in_specs=[pl.BlockSpec(memory_space=pltpu.SMEM)] + [vmem] * (1 + len(sides)),
         out_specs=vmem,
-        out_shape=jax.ShapeDtypeStruct((solved.shape[0], count), jnp.float32),
+        out_shape=jax.ShapeDtypeStruct((solved.shape[0], total), jnp.float32),
         name="score",
-    )(side, solved, *blocks)
+    )(side, solved, *sides)
 
 
 def after(x, *others):
@@ -492,13 +492,13 @@
             for step in steps[:-1]:
                 near = near[:1] + [lax.ppermute(x, "dp", step) for x in near]
         if c == 3 and steps:
-            near = list(lax.optimization_barrier((*near, out[0])))[:-1]
-            near += [lax.ppermute(x, "dp", steps[-1]) for x in near]
+            near = jnp.concatenate(near[:1] + [after(x, out[0]) for x in near[1:]], axis=0)
+            near = [near, lax.ppermute(near, "dp", steps[-1])]
         if c < count - 1:
             x_rows, *out = out
             state.append(out)
     side = (dp >= seqs // 2).astype(jnp.int32).reshape(1)
-    scores = from_middle(score(side, out[0], near))
+    scores = from_middle(score(query_grads.shape[2], side, out[0], near))
     mine = lax.dynamic_slice(scores, (dp, 0), (1, scores.shape[1]))
     if lax.axis_size("mod") == 2:
         return mine + lax.ppermute(mine, "mod", SWAP)

time: 120 us -> 122 us (1.017)
  starting transfers between devices: 39 us -> 35.5 us
  Pallas kernels: 52.5 us -> 55.5 us
  waiting for transfers between devices: 11.2 us -> 12.6 us
    pallas_call x5, Pallas kernels: 43.2 us -> 46.3 us  [panel(): pl.pallas_call(functools.partial(panel_kernel, c, size, seqs, padded), in...]
    ppermute x1, starting transfers between devices: 6 us -> 2.96 us  [body(): near = near[:1] + [lax.ppermute(x, 'dp', step) for x in near]]
    ppermute x8, waiting for transfers between devices: 1.51 us -> 2.9 us  [body(): others = [lax.ppermute(half, 'rep', SWAP) for half in (x, got)]]
    unnamed x36 -> x39, local copies, waits for them, and re-layouts: 4.28 us -> 4.93 us
  transfers between devices with their start and end apart: 28 -> 27, of which waited for: 6 -> 8; matrix products, arithmetic and copies ran while one was open for 8% -> 8% of each run, Pallas kernels for 36% -> 38%
where the time goes in v3:
time: 122 us; the launch traced here: 121 us
  Pallas kernels  55.5 us (45%)
  starting transfers between devices  35.5 us (29%)
  waiting for transfers between devices  12.6 us (10%)
  local copies, waits for them, and re-layouts  8.92 us (7%)
  other arithmetic  7.06 us (6%)
    pallas_call x5, Pallas kernels, panel(): pl.pallas_call(functools.partial(panel_kernel, c, size, seqs, padded), in...  46.3 us
    ppermute x4, starting transfers between devices, inwards(): x = x + after(lax.ppermute(x, 'dp', step), *gate)  17 us
    pallas_call x1, Pallas kernels, project(): pl.pallas_call(functools.partial(project_kernel, steps, seqs), grid=(step...  6.89 us
    ppermute x1, waiting for transfers between devices, from_middle(): got = lax.ppermute(x, 'dp', [(s + 1, s), (n - 2 - s, n - 1 - s)])  5.73 us
    ppermute x2, starting transfers between devices, body(): first = first + lax.ppermute(first, 'dp', step)  5.53 us
    unnamed x39, local copies, waits for them, and re-layouts  4.93 us
    dynamic_slice x4, local copies, waits for them, and re-layouts, over_rep(): other = lax.dynamic_slice(array, (top + (1 - rep) * half, 0), (half, wide))  3.97 us
    ppermute x4, starting transfers between devices, body(): got = lax.ppermute(x, 'dp', steps[-1]) if steps else jnp.zeros_like(x)  3.25 us
  transfers between devices with their start and end apart: 27, of which 8 were waited for; matrix products, arithmetic and copies ran while one was open for 8% of the time, Pallas kernels for 38%

profile of v3, /device:TPU:0, one launch (start us, length us, event | category | flops | bytes accessed | tf_op | source)
XLA Modules:
  0.0 120.6 jit_solution(10774420774825435778)
XLA Ops:
  0.7 0.6 pad_add_fusion.place_ref
  1.3 6.9 %project.1 = f32[168,128]{1,0:T(8,128)} custom-call(s32[3]{0:T(128)} %pad_add_fusion.place_ref, bf16[1,1,512,4096]{3,2,1,0:T(8,128)(2,1)} %act_ref.1, bf16[1,1,512,4096]{3,2,1,0:T(8,128)(2,1)} %grad_ref.1, bf16[1,32,4096]{2,1,0:T(8,128)(2,1)} %pin_ref.1, bf16[1,32,4096]{2,1,0:T(8,128)(2,1)} %pout_ref.1, f32[1,1,1024,1024]{3,2,1,0:T(8,128)} %prior_ref.1), custom_call_target="tpu_custom_call" | custom-call | tf_op jit(solution)/shard_map/project/pallas_call | solution.py:110
  8.2 0.5 collective-permute-start
  8.6 0.9 dynamic-slice_bitcast_fusion
  9.7 0.9 add.103
  10.6 4.9 %collective-permute-start.2 = (f32[168,128]{1,0:T(8,128)S(1)}, f32[168,128]{1,0:T(8,128)S(1)}, u32[]{:S(2)}, u32[]{:S(2)}) collective-permute-start(f32[168,128]{1,0:T(8,128)S(1)} %add.103), channel_id=1, source_target_pairs={{0,4},{12,8},{1,5},{13,9},{2,6},{14,10},{3,7},{15,11},{16,20},{28,... | collective-permute-start | bytes 258056 | tf_op jit(solution)/shard_map/ppermute | solution.py:462
  15.5 1.1 constant_dynamic-slice_fusion.2
  16.7 1.0 constant_dynamic-slice_fusion.3
  17.7 0.6 collective-permute-start.6
  18.2 1.0 constant_dynamic-slice_fusion.4
  19.3 0.7 collective-permute-start.9
  20.0 1.0 bitcast_add_fusion
  20.9 5.5 %collective-permute-start.5 = (f32[128,384]{1,0:T(8,128)S(1)}, f32[128,384]{1,0:T(8,128)S(1)}, u32[]{:S(2)}, u32[]{:S(2)}) collective-permute-start(f32[128,384]{1,0:T(8,128)S(1)} %bitcast_add_fusion), channel_id=1, source_target_pairs={{0,4},{12,8},{1,5},{13,9},{2,6},{14,10},{3,7},{15,11},{16,20},{28,... | collective-permute-start | bytes 589832 | tf_op jit(solution)/shard_map/ppermute | solution.py:470
  26.5 1.0 dynamic-slice_add_fusion.1
  27.5 1.3 %collective-permute-start.15 = (f32[128,640]{1,0:T(8,128)S(1)}, f32[128,640]{1,0:T(8,128)S(1)}, u32[]{:S(2)}, u32[]{:S(2)}) collective-permute-start(f32[128,640]{1,0:T(8,128)S(1)} %dynamic-slice_add_fusion.1), channel_id=1, source_target_pairs={{0,4},{12,8},{1,5},{13,9},{2,6},{14,10},{3,7},{15,11},{16,20},{28,... | collective-permute-start | bytes 983048 | tf_op jit(solution)/shard_map/ppermute | solution.py:470
  28.8 1.1 dynamic-slice_add_fusion
  29.9 1.7 %collective-permute-done.5 = f32[128,384]{1,0:T(8,128)S(1)} collective-permute-done((f32[128,384]{1,0:T(8,128)S(1)}, f32[128,384]{1,0:T(8,128)S(1)}, u32[]{:S(2)}, u32[]{:S(2)}) %collective-permute-start.5) | collective-permute-done | bytes 196640 | tf_op jit(solution)/shard_map/ppermute | solution.py:470
  31.7 0.7 collective-permute-start.8
  32.5 6.1 %collective-permute-start.13 = (f32[128,896]{1,0:T(8,128)S(1)}, f32[128,896]{1,0:T(8,128)S(1)}, u32[]{:S(2)}, u32[]{:S(2)}) collective-permute-start(f32[128,896]{1,0:T(8,128)S(1)} %dynamic-slice_add_fusion), channel_id=1, source_target_pairs={{0,4},{12,8},{1,5},{13,9},{2,6},{14,10},{3,7},{15,11},{16,20},{28,... | collective-permute-start | bytes 1376264 | tf_op jit(solution)/shard_map/ppermute | solution.py:470
  38.6 3.5 %panel0.1 = (f32[16,1024]{1,0:T(8,128)S(1)}, f32[8,128]{1,0:T(8,128)S(1)}, bf16[256,384]{1,0:T(8,128)(2,1)S(1)}, f32[128,128]{1,0:T(8,128)S(1)}) custom-call(f32[168,128]{1,0:T(8,128)S(1)} %add.126.refs_0_), custom_call_target="tpu_custom_call" | custom-call | flops 1200000000 | bytes 4000000 | tf_op jit(solution)/shard_map/panel0/pallas_call | solution.py:374
  42.1 0.7 collective-permute-start.16
  43.1 1.0 dynamic-slice_add_fusion.2
  44.1 4.1 %collective-permute-start.3 = (f32[64,1024]{1,0:T(8,128)S(1)}, f32[64,1024]{1,0:T(8,128)S(1)}, u32[]{:S(2)}, u32[]{:S(2)}) collective-permute-start(f32[64,1024]{1,0:T(8,128)S(1)} %dynamic-slice_add_fusion.2), channel_id=1, source_target_pairs={{0,4},{12,8},{1,5},{13,9},{2,6},{14,10},{3,7},{15,11},{16,20},{28,... | collective-permute-start | bytes 786440 | tf_op jit(solution)/shard_map/ppermute | solution.py:470
  48.2 7.2 %panel1.1 = (f32[8,384]{1,0:T(8,128)S(1)}, bf16[1024,384]{1,0:T(8,128)(2,1)S(1)}, f32[256,384]{1,0:T(8,128)S(1)}) custom-call(s32[1]{0:T(128)} %bitcast.1.refs_0_, f32[128,384]{1,0:T(8,128)S(1)} %add.125.refs_1_, f32[128,384]{1,0:T(8,128)S(1)} %collective-permute-done.8.refs_2_, f32[128,384]{1,0:T(8,128)S(1)} %collective-permute-done.10.refs_3_, ...), custom_call_target="tpu_custom_call" | custom-call | flops 1200000000 | bytes 4000000 | tf_op jit(solution)/shard_map/panel1/pallas_call | solution.py:374
  55.5 1.0 collective-permute-start.14
  56.6 0.5 collective-permute-start.18
  57.2 1.0 collective-permute-done.17.refs_3_
  58.2 0.5 collective-permute-done.18.refs_4_
  58.7 8.7 %panel2.1 = (f32[8,640]{1,0:T(8,128)S(1)}, bf16[1536,384]{1,0:T(8,128)(2,1)S(1)}, f32[256,640]{1,0:T(8,128)S(1)}) custom-call(s32[1]{0:T(128)} %bitcast.1.refs_0_, f32[128,640]{1,0:T(8,128)S(1)} %add.129.refs_1_, f32[128,640]{1,0:T(8,128)S(1)} %collective-permute-done.16.refs_2_, f32[128,640]{1,0:T(8,128)S(1)} %collective-permute-done.17.refs_3_, ...), custom_call_target="tpu_custom_call" | custom-call | flops 1200000000 | bytes 4000000 | tf_op jit(solution)/shard_map/panel2/pallas_call | solution.py:374
  67.4 1.0 copy-done
  68.5 0.9 copy-done.2
  69.3 0.6 copy-done.7
  70.1 3.0 %collective-permute-start.23 = (bf16[128,1024]{1,0:T(8,128)(2,1)S(1)}, bf16[128,1024]{1,0:T(8,128)(2,1)S(1)}, u32[]{:S(2)}, u32[]{:S(2)}) collective-permute-start(bf16[128,1024]{1,0:T(8,128)(2,1)S(1)} %bitcast.16), channel_id=1, source_target_pairs={{0,4},{12,8},{1,5},{13,9},{2,6},{14,10},{3,7},{15,11},{16,20},{28,... | collective-permute-start | bytes 786440 | tf_op jit(solution)/shard_map/ppermute | solution.py:493
  73.0 0.9 collective-permute-start.12
  74.0 0.8 copy-done.18
  74.9 13.4 %panel3.1 = (f32[8,896]{1,0:T(8,128)}, bf16[2048,384]{1,0:T(8,128)(2,1)}, f32[256,896]{1,0:T(8,128)}) custom-call(s32[1]{0:T(128)} %bitcast.1.refs_0_, f32[128,896]{1,0:T(8,128)} %copy-done.11, f32[128,896]{1,0:T(8,128)} %copy-done.16, f32[128,896]{1,0:T(8,128)} %copy-done.17, f32[128,896]{1,0:T(8,128)} %copy-done.18, f32[16,1024]{1,0:T(8,128)} %copy-done.5, ...), custom_call_target="tpu_custom_call" | custom-call | flops 1200000000 | bytes 4000000 | tf_op jit(solution)/shard_map/panel3/pallas_call | solution.py:374
  88.3 1.0 collective-permute-start.24
  89.4 0.4 collective-permute-start.22
  89.9 1.0 collective-permute-done.21.refs_3_
  92.0 13.6 %panel4.1.solved_ref = f32[8,1024]{1,0:T(8,128)} custom-call(s32[1]{0:T(128)} %bitcast.1.refs_0_, f32[64,1024]{1,0:T(8,128)} %copy-done.9, f32[64,1024]{1,0:T(8,128)} %copy-done.12, f32[64,1024]{1,0:T(8,128)} %copy-done.13, f32[64,1024]{1,0:T(8,128)} %copy-done.14, f32[16,1024]{1,0:T(8,128)} %copy-done.5, f32[8,896]{1,0:T(8,128)} %get-tuple-element.56.refs_6_, ...), custom_call_target="tpu_custom_call" | custom-call | flops 1200000000 | bytes 4000000 | tf_op jit(solution)/shard_map/panel4/pallas_call | solution.py:374
  105.6 0.8 copy-done.10
  106.4 2.3 %score.1 = f32[8,512]{1,0:T(8,128)} custom-call(s32[1]{0:T(128)} %bitcast.side_ref, f32[8,1024]{1,0:T(8,128)} %panel4.1.solved_ref, bf16[256,1024]{1,0:T(8,128)(2,1)} %copy-done.8, bf16[256,1024]{1,0:T(8,128)(2,1)} %copy-done.10), custom_call_target="tpu_custom_call" | custom-call | tf_op jit(solution)/shard_map/score/pallas_call | solution.py:409
  108.7 1.3 %collective-permute-start.25 = (f32[8,512]{1,0:T(8,128)}, f32[8,512]{1,0:T(8,128)S(1)}, u32[]{:S(2)}, u32[]{:S(2)}) collective-permute-start(f32[8,512]{1,0:T(8,128)} %score.1), channel_id=1, source_target_pairs={{4,0},{8,12},{5,1},{9,13},{6,2},{10,14},{7,3},{11,15},{20,16},{24,... | collective-permute-start | bytes 49160 | tf_op jit(solution)/shard_map/ppermute | solution.py:431
  110.0 5.7 %collective-permute-done.25 = f32[8,512]{1,0:T(8,128)S(1)} collective-permute-done((f32[8,512]{1,0:T(8,128)}, f32[8,512]{1,0:T(8,128)S(1)}, u32[]{:S(2)}, u32[]{:S(2)}) %collective-permute-start.25) | collective-permute-done | bytes 16416 | tf_op jit(solution)/shard_map/ppermute | solution.py:431
  115.7 0.7 broadcast_select_fusion
  116.5 1.5 %collective-permute-start.26 = (f32[1,512]{1,0:T(1,128)S(1)}, f32[1,512]{1,0:T(1,128)S(1)}, u32[]{:S(2)}, u32[]{:S(2)}) collective-permute-start(f32[1,512]{1,0:T(1,128)S(1)} %broadcast_select_fusion), channel_id=1, source_target_pairs={{0,2},{2,0},{1,3},{3,1},{4,6},{6,4},{5,7},{7,5},{8,10},{10,8},{9,1... | collective-permute-start | bytes 6152 | tf_op jit(solution)/shard_map/ppermute | solution.py:504
  117.9 2.1 %collective-permute-done.26 = f32[1,512]{1,0:T(1,128)S(1)} collective-permute-done((f32[1,512]{1,0:T(1,128)S(1)}, f32[1,512]{1,0:T(1,128)S(1)}, u32[]{:S(2)}, u32[]{:S(2)}) %collective-permute-start.26) | collective-permute-done | bytes 2080 | tf_op jit(solution)/shard_map/ppermute | solution.py:504
  120.0 0.6 add.131
  (71 shorter events, 2.7 us)
Async XLA Ops:
  8.2 1.6 %collective-permute-start = (f32[168,128]{1,0:T(8,128)}, f32[168,128]{1,0:T(8,128)S(1)}, u32[]{:S(2)}, u32[]{:S(2)}) collective-permute-start(f32[168,128]{1,0:T(8,128)} %project.1), channel_id=1, source_target_pairs={{0,1},{1,0},{2,3},{3,2},{4,5},{5,4},{6,7},{7,6},{8,9},{9,8},{10,11... | collective-permute-start | bytes 258056 | tf_op jit(solution)/shard_map/ppermute | solution.py:459
  9.5 10.4 %collective-permute-start.4 = (f32[128,384]{1,0:T(8,128)S(1)}, f32[128,384]{1,0:T(8,128)S(1)}, u32[]{:S(2)}, u32[]{:S(2)}) collective-permute-start(f32[128,384]{1,0:T(8,128)S(1)} %dynamic-slice_bitcast_fusion), channel_id=1, source_target_pairs={{0,1},{1,0},{2,3},{3,2},{4,5},{5,4},{6,7},{7,6},{8,9},{9,8},{10,11... | collective-permute-start | bytes 589832 | tf_op jit(solution)/shard_map/ppermute | solution.py:454
  10.6 8.6 %collective-permute-start.2 = (f32[168,128]{1,0:T(8,128)S(1)}, f32[168,128]{1,0:T(8,128)S(1)}, u32[]{:S(2)}, u32[]{:S(2)}) collective-permute-start(f32[168,128]{1,0:T(8,128)S(1)} %add.103), channel_id=1, source_target_pairs={{0,4},{12,8},{1,5},{13,9},{2,6},{14,10},{3,7},{15,11},{16,20},{28,... | collective-permute-start | bytes 258056 | tf_op jit(solution)/shard_map/ppermute | solution.py:462
  16.6 12.2 %collective-permute-start.7 = (f32[128,896]{1,0:T(8,128)S(1)}, f32[128,896]{1,0:T(8,128)S(1)}, u32[]{:S(2)}, u32[]{:S(2)}) collective-permute-start(f32[128,896]{1,0:T(8,128)S(1)} %constant_dynamic-slice_fusion.2), channel_id=1, source_target_pairs={{0,1},{1,0},{2,3},{3,2},{4,5},{5,4},{6,7},{7,6},{8,9},{9,8},{10,11... | collective-permute-start | bytes 1376264 | tf_op jit(solution)/shard_map/ppermute | solution.py:454
  17.7 8.8 %collective-permute-start.6 = (f32[128,640]{1,0:T(8,128)S(1)}, f32[128,640]{1,0:T(8,128)S(1)}, u32[]{:S(2)}, u32[]{:S(2)}) collective-permute-start(f32[128,640]{1,0:T(8,128)S(1)} %constant_dynamic-slice_fusion.3), channel_id=1, source_target_pairs={{0,1},{1,0},{2,3},{3,2},{4,5},{5,4},{6,7},{7,6},{8,9},{9,8},{10,11... | collective-permute-start | bytes 983048 | tf_op jit(solution)/shard_map/ppermute | solution.py:454
  19.2 23.9 %collective-permute-start.1 = (f32[64,1024]{1,0:T(8,128)S(1)}, f32[64,1024]{1,0:T(8,128)S(1)}, u32[]{:S(2)}, u32[]{:S(2)}) collective-permute-start(f32[64,1024]{1,0:T(8,128)S(1)} %constant_dynamic-slice_fusion.4), channel_id=1, source_target_pairs={{0,1},{1,0},{2,3},{3,2},{4,5},{5,4},{6,7},{7,6},{8,9},{9,8},{10,11... | collective-permute-start | bytes 786440 | tf_op jit(solution)/shard_map/ppermute | solution.py:454
  19.3 13.1 %collective-permute-start.9 = (f32[168,128]{1,0:T(8,128)S(1)}, f32[168,128]{1,0:T(8,128)S(1)}, u32[]{:S(2)}, u32[]{:S(2)}) collective-permute-start(f32[168,128]{1,0:T(8,128)S(1)} %add.109), channel_id=1, source_target_pairs={{4,8},{8,4},{5,9},{9,5},{6,10},{10,6},{7,11},{11,7},{20,24},{24,20... | collective-permute-start | bytes 258056 | tf_op jit(solution)/shard_map/ppermute | solution.py:462
  20.9 10.7 %collective-permute-start.5 = (f32[128,384]{1,0:T(8,128)S(1)}, f32[128,384]{1,0:T(8,128)S(1)}, u32[]{:S(2)}, u32[]{:S(2)}) collective-permute-start(f32[128,384]{1,0:T(8,128)S(1)} %bitcast_add_fusion), channel_id=1, source_target_pairs={{0,4},{12,8},{1,5},{13,9},{2,6},{14,10},{3,7},{15,11},{16,20},{28,... | collective-permute-start | bytes 589832 | tf_op jit(solution)/shard_map/ppermute | solution.py:470
  27.5 14.5 %collective-permute-start.15 = (f32[128,640]{1,0:T(8,128)S(1)}, f32[128,640]{1,0:T(8,128)S(1)}, u32[]{:S(2)}, u32[]{:S(2)}) collective-permute-start(f32[128,640]{1,0:T(8,128)S(1)} %dynamic-slice_add_fusion.1), channel_id=1, source_target_pairs={{0,4},{12,8},{1,5},{13,9},{2,6},{14,10},{3,7},{15,11},{16,20},{28,... | collective-permute-start | bytes 983048 | tf_op jit(solution)/shard_map/ppermute | solution.py:470
  31.7 11.1 %collective-permute-start.8 = (f32[128,384]{1,0:T(8,128)S(1)}, f32[128,384]{1,0:T(8,128)S(1)}, u32[]{:S(2)}, u32[]{:S(2)}) collective-permute-start(f32[128,384]{1,0:T(8,128)S(1)} %add.125.refs_1_), channel_id=1, source_target_pairs={{4,8},{8,4},{5,9},{9,5},{6,10},{10,6},{7,11},{11,7},{20,24},{24,20... | collective-permute-start | bytes 589832 | tf_op jit(solution)/shard_map/ppermute | solution.py:483
  32.4 15.8 %collective-permute-start.10 = (f32[128,384]{1,0:T(8,128)S(1)}, f32[128,384]{1,0:T(8,128)S(1)}, u32[]{:S(2)}, u32[]{:S(2)}) collective-permute-start(f32[128,384]{1,0:T(8,128)S(1)} %add.125.refs_1_), channel_id=1, source_target_pairs={{0,1},{1,0},{2,3},{3,2},{4,5},{5,4},{6,7},{7,6},{8,9},{9,8},{10,11... | collective-permute-start | bytes 589832 | tf_op jit(solution)/shard_map/ppermute | solution.py:487
  32.5 22.9 %collective-permute-start.13 = (f32[128,896]{1,0:T(8,128)S(1)}, f32[128,896]{1,0:T(8,128)S(1)}, u32[]{:S(2)}, u32[]{:S(2)}) collective-permute-start(f32[128,896]{1,0:T(8,128)S(1)} %dynamic-slice_add_fusion), channel_id=1, source_target_pairs={{0,4},{12,8},{1,5},{13,9},{2,6},{14,10},{3,7},{15,11},{16,20},{28,... | collective-permute-start | bytes 1376264 | tf_op jit(solution)/shard_map/ppermute | solution.py:470
  42.0 25.4 %copy-start.4 = (bf16[256,384]{1,0:T(8,128)(2,1)}, bf16[256,384]{1,0:T(8,128)(2,1)S(1)}, u32[]{:S(2)}) copy-start(bf16[256,384]{1,0:T(8,128)(2,1)S(1)} %get-tuple-element.45.refs_7_) | copy-start | bytes 589828
  42.0 25.4 %copy-start.5 = (f32[16,1024]{1,0:T(8,128)}, f32[16,1024]{1,0:T(8,128)S(1)}, u32[]{:S(2)}) copy-start(f32[16,1024]{1,0:T(8,128)S(1)} %get-tuple-element.42.refs_5_) | copy-start | bytes 196612
  42.0 25.4 %copy-start.6 = (f32[128,128]{1,0:T(8,128)}, f32[128,128]{1,0:T(8,128)S(1)}, u32[]{:S(2)}) copy-start(f32[128,128]{1,0:T(8,128)S(1)} %get-tuple-element.59.refs_11_) | copy-start | bytes 196612
  42.1 14.5 %collective-permute-start.16 = (f32[128,640]{1,0:T(8,128)S(1)}, f32[128,640]{1,0:T(8,128)S(1)}, u32[]{:S(2)}, u32[]{:S(2)}) collective-permute-start(f32[128,640]{1,0:T(8,128)S(1)} %add.129.refs_1_), channel_id=1, source_target_pairs={{4,8},{8,4},{5,9},{9,5},{6,10},{10,6},{7,11},{11,7},{20,24},{24,20... | collective-permute-start | bytes 983048 | tf_op jit(solution)/shard_map/ppermute | solution.py:483
  42.8 5.4 %collective-permute-start.11 = (f32[128,384]{1,0:T(8,128)S(1)}, f32[128,384]{1,0:T(8,128)S(1)}, u32[]{:S(2)}, u32[]{:S(2)}) collective-permute-start(f32[128,384]{1,0:T(8,128)S(1)} %collective-permute-done.8.refs_2_), channel_id=1, source_target_pairs={{0,1},{1,0},{2,3},{3,2},{4,5},{5,4},{6,7},{7,6},{8,9},{9,8},{10,11... | collective-permute-start | bytes 589832 | tf_op jit(solution)/shard_map/ppermute | solution.py:487
  44.1 12.4 %collective-permute-start.3 = (f32[64,1024]{1,0:T(8,128)S(1)}, f32[64,1024]{1,0:T(8,128)S(1)}, u32[]{:S(2)}, u32[]{:S(2)}) collective-permute-start(f32[64,1024]{1,0:T(8,128)S(1)} %dynamic-slice_add_fusion.2), channel_id=1, source_target_pairs={{0,4},{12,8},{1,5},{13,9},{2,6},{14,10},{3,7},{15,11},{16,20},{28,... | collective-permute-start | bytes 786440 | tf_op jit(solution)/shard_map/ppermute | solution.py:470
  55.4 3.3 %copy-start.3 = (f32[256,384]{1,0:T(8,128)}, f32[256,384]{1,0:T(8,128)S(1)}, u32[]{:S(2)}) copy-start(f32[256,384]{1,0:T(8,128)S(1)} %get-tuple-element.60.refs_12_) | copy-start | bytes 1179652
  55.4 19.4 %copy-start.1 = (bf16[1024,384]{1,0:T(8,128)(2,1)}, bf16[1024,384]{1,0:T(8,128)(2,1)S(1)}, u32[]{:S(2)}) copy-start(bf16[1024,384]{1,0:T(8,128)(2,1)S(1)} %get-tuple-element.52.refs_8_) | copy-start | bytes 2359300
  55.4 14.7 %copy-start.15 = (bf16[1,1,128,1024]{3,2,1,0:T(8,128)(2,1)S(1)}, bf16[1,1,128,1024]{3,2,1,0:T(8,128)(2,1)}, u32[]{:S(2)}) copy-start(bf16[1,1,128,1024]{3,2,1,0:T(8,128)(2,1)} %param.13) | copy-start | bytes 786436
  55.5 19.4 %copy-start.11 = (f32[128,896]{1,0:T(8,128)}, f32[128,896]{1,0:T(8,128)S(1)}, u32[]{:S(2)}) copy-start(f32[128,896]{1,0:T(8,128)S(1)} %add.128.refs_1_) | copy-start | bytes 1376260
  55.5 14.5 %collective-permute-start.14 = (f32[128,896]{1,0:T(8,128)S(1)}, f32[128,896]{1,0:T(8,128)S(1)}, u32[]{:S(2)}, u32[]{:S(2)}) collective-permute-start(f32[128,896]{1,0:T(8,128)S(1)} %add.128.refs_1_), channel_id=1, source_target_pairs={{4,8},{8,4},{5,9},{9,5},{6,10},{10,6},{7,11},{11,7},{20,24},{24,20... | collective-permute-start | bytes 1376264 | tf_op jit(solution)/shard_map/ppermute | solution.py:483
  56.5 32.8 %copy-start.9 = (f32[64,1024]{1,0:T(8,128)}, f32[64,1024]{1,0:T(8,128)S(1)}, u32[]{:S(2)}) copy-start(f32[64,1024]{1,0:T(8,128)S(1)} %add.127.refs_1_) | copy-start | bytes 786436
  56.5 1.7 %collective-permute-start.17 = (f32[128,640]{1,0:T(8,128)S(1)}, f32[128,640]{1,0:T(8,128)S(1)}, u32[]{:S(2)}, u32[]{:S(2)}) collective-permute-start(f32[128,640]{1,0:T(8,128)S(1)} %add.129.refs_1_), channel_id=1, source_target_pairs={{0,1},{1,0},{2,3},{3,2},{4,5},{5,4},{6,7},{7,6},{8,9},{9,8},{10,11... | collective-permute-start | bytes 983048 | tf_op jit(solution)/shard_map/ppermute | solution.py:487
  56.6 2.1 %collective-permute-start.18 = (f32[128,640]{1,0:T(8,128)S(1)}, f32[128,640]{1,0:T(8,128)S(1)}, u32[]{:S(2)}, u32[]{:S(2)}) collective-permute-start(f32[128,640]{1,0:T(8,128)S(1)} %collective-permute-done.16.refs_2_), channel_id=1, source_target_pairs={{0,1},{1,0},{2,3},{3,2},{4,5},{5,4},{6,7},{7,6},{8,9},{9,8},{10,11... | collective-permute-start | bytes 983048 | tf_op jit(solution)/shard_map/ppermute | solution.py:487
  57.1 16.8 %collective-permute-start.19 = (f32[128,896]{1,0:T(8,128)S(1)}, f32[128,896]{1,0:T(8,128)S(1)}, u32[]{:S(2)}, u32[]{:S(2)}) collective-permute-start(f32[128,896]{1,0:T(8,128)S(1)} %add.128.refs_1_), channel_id=1, source_target_pairs={{0,1},{1,0},{2,3},{3,2},{4,5},{5,4},{6,7},{7,6},{8,9},{9,8},{10,11... | collective-permute-start | bytes 1376264 | tf_op jit(solution)/shard_map/ppermute | solution.py:487
  67.4 1.0 copy-start
  68.5 0.9 copy-start.2
  69.3 0.6 copy-start.7
  69.9 4.9 %copy-start.16 = (f32[128,896]{1,0:T(8,128)}, f32[128,896]{1,0:T(8,128)S(1)}, u32[]{:S(2)}) copy-start(f32[128,896]{1,0:T(8,128)S(1)} %collective-permute-done.14.refs_2_) | copy-start | bytes 1376260
  69.9 4.1 %collective-permute-start.20 = (f32[128,896]{1,0:T(8,128)S(1)}, f32[128,896]{1,0:T(8,128)S(1)}, u32[]{:S(2)}, u32[]{:S(2)}) collective-permute-start(f32[128,896]{1,0:T(8,128)S(1)} %collective-permute-done.14.refs_2_), channel_id=1, source_target_pairs={{0,1},{1,0},{2,3},{3,2},{4,5},{5,4},{6,7},{7,6},{8,9},{9,8},{10,11... | collective-permute-start | bytes 1376264 | tf_op jit(solution)/shard_map/ppermute | solution.py:487
  70.1 18.2 %collective-permute-start.23 = (bf16[128,1024]{1,0:T(8,128)(2,1)S(1)}, bf16[128,1024]{1,0:T(8,128)(2,1)S(1)}, u32[]{:S(2)}, u32[]{:S(2)}) collective-permute-start(bf16[128,1024]{1,0:T(8,128)(2,1)S(1)} %bitcast.16), channel_id=1, source_target_pairs={{0,4},{12,8},{1,5},{13,9},{2,6},{14,10},{3,7},{15,11},{16,20},{28,... | collective-permute-start | bytes 786440 | tf_op jit(solution)/shard_map/ppermute | solution.py:493
  73.0 16.4 %collective-permute-start.12 = (f32[64,1024]{1,0:T(8,128)S(1)}, f32[64,1024]{1,0:T(8,128)S(1)}, u32[]{:S(2)}, u32[]{:S(2)}) collective-permute-start(f32[64,1024]{1,0:T(8,128)S(1)} %add.127.refs_1_), channel_id=1, source_target_pairs={{4,8},{8,4},{5,9},{9,5},{6,10},{10,6},{7,11},{11,7},{20,24},{24,20... | collective-permute-start | bytes 786440 | tf_op jit(solution)/shard_map/ppermute | solution.py:483
  74.0 0.9 copy-start.17
  74.0 0.8 copy-start.18
  88.3 17.3 %copy-start.8 = (bf16[256,1024]{1,0:T(8,128)(2,1)}, bf16[256,1024]{1,0:T(8,128)(2,1)S(1)}, u32[]{:S(2)}) copy-start(bf16[256,1024]{1,0:T(8,128)(2,1)S(1)} %constant_dynamic-update-slice_fusion.refs_0_) | copy-start | bytes 1572868
  88.3 17.3 %collective-permute-start.24 = (bf16[256,1024]{1,0:T(8,128)(2,1)S(1)}, bf16[256,1024]{1,0:T(8,128)(2,1)S(1)}, u32[]{:S(2)}, u32[]{:S(2)}) collective-permute-start(bf16[256,1024]{1,0:T(8,128)(2,1)S(1)} %constant_dynamic-update-slice_fusion.refs_0_), channel_id=1, source_target_pairs={{4,8},{8,4},{5,9},{9,5},{6,10},{10,6},{7,11},{11,7},{20,24},{24,20... | collective-permute-start | bytes 1572872 | tf_op jit(solution)/shard_map/ppermute | solution.py:496
  89.3 1.6 %collective-permute-start.21 = (f32[64,1024]{1,0:T(8,128)S(1)}, f32[64,1024]{1,0:T(8,128)S(1)}, u32[]{:S(2)}, u32[]{:S(2)}) collective-permute-start(f32[64,1024]{1,0:T(8,128)S(1)} %add.127.refs_1_), channel_id=1, source_target_pairs={{0,1},{1,0},{2,3},{3,2},{4,5},{5,4},{6,7},{7,6},{8,9},{9,8},{10,11... | collective-permute-start | bytes 786440 | tf_op jit(solution)/shard_map/ppermute | solution.py:487
  89.4 1.8 %copy-start.12 = (f32[64,1024]{1,0:T(8,128)}, f32[64,1024]{1,0:T(8,128)S(1)}, u32[]{:S(2)}) copy-start(f32[64,1024]{1,0:T(8,128)S(1)} %collective-permute-done.12.refs_2_) | copy-start | bytes 786436
  89.4 1.8 %collective-permute-start.22 = (f32[64,1024]{1,0:T(8,128)S(1)}, f32[64,1024]{1,0:T(8,128)S(1)}, u32[]{:S(2)}, u32[]{:S(2)}) collective-permute-start(f32[64,1024]{1,0:T(8,128)S(1)} %collective-permute-done.12.refs_2_), channel_id=1, source_target_pairs={{0,1},{1,0},{2,3},{3,2},{4,5},{5,4},{6,7},{7,6},{8,9},{9,8},{10,11... | collective-permute-start | bytes 786440 | tf_op jit(solution)/shard_map/ppermute | solution.py:487
  90.9 0.7 copy-start.13
  91.3 0.7 copy-start.14
  105.6 0.8 copy-start.10
  108.7 7.0 %collective-permute-start.25 = (f32[8,512]{1,0:T(8,128)}, f32[8,512]{1,0:T(8,128)S(1)}, u32[]{:S(2)}, u32[]{:S(2)}) collective-permute-start(f32[8,512]{1,0:T(8,128)} %score.1), channel_id=1, source_target_pairs={{4,0},{8,12},{5,1},{9,13},{6,2},{10,14},{7,3},{11,15},{20,16},{24,... | collective-permute-start | bytes 49160 | tf_op jit(solution)/shard_map/ppermute | solution.py:431
  116.5 3.6 %collective-permute-start.26 = (f32[1,512]{1,0:T(1,128)S(1)}, f32[1,512]{1,0:T(1,128)S(1)}, u32[]{:S(2)}, u32[]{:S(2)}) collective-permute-start(f32[1,512]{1,0:T(1,128)S(1)} %broadcast_select_fusion), channel_id=1, source_target_pairs={{0,2},{2,0},{1,3},{3,1},{4,6},{6,4},{5,7},{7,5},{8,10},{10,8},{9,1... | collective-permute-start | bytes 6152 | tf_op jit(solution)/shard_map/ppermute | solution.py:504
